TPU v7x, 512 devices: a whole 4x4x16 slice. The times are simulated.
512 devices in a mesh: kcol: 128 (over y, z, core), band: 4 (over x).
Axes of the slice: x: 4, y: 4, z: 16, core: 2. Of those that a mesh axis runs over, the one named last changes fastest.
Arguments:
- coarse_kernel: bfloat16 [576, 73728], P('band', 'kcol'), may hold values from -6 to 6
- row_intersection: float32 [2, 4, 8, 12], P(None, 'band'), may hold values from -1.75 to 1.75
- col_intersection: float32 [2, 18432, 8, 12], P(None, 'kcol'), may hold values from -1.75 to 1.75
- row_nearest: int32 [4], P('band'), may hold values from 0 to 3
- col_nearest: int32 [18432], P('kcol'), may hold values from 0 to 511, as said below
- qp_energy: float32 [256], P('band'), may hold values from 1 to 4
Outputs:
- fine_kernel: bfloat16 [256, 1179648], P('band', 'kcol')
Inputs may be any that keep to these rules, and one draw needn't show every extreme that they name: `col_nearest`: coarse point c is held by index c // 4 of kcol. Among the 144 fine points held by one index of kcol, at most 2 have nearest coarse points held by any one index of kcol; in every draw one index of kcol is the holder for exactly 2 fine points of every index.
All inputs are finite; a program needn't handle non-finite values.
Results may differ from a plain program's by a relative error of at most 0.0012.
The roundings to bfloat16 on the way count: a program that leaves them out, or rounds other values in their place, can miss the bound.
Values may be sent and summed in bfloat16 or wider, within the bound.
No kernel may reach another device: no remote copies, remote signals or barrier semaphores. Data moves between devices by JAX's collectives and lax.ppermute only.
A program may use at most 192 MiB of HBM per device.

v0:
```python
import jax
import jax.numpy as jnp
from jax import lax
from jax.sharding import PartitionSpec as P

NBF = 8
NBC = 12
RC = 4


def pair_coefficient(intersection):
    conduction = intersection[0]
    valence = intersection[1]
    points = conduction.shape[0]
    fine_bands = conduction.shape[1]
    coarse_bands = conduction.shape[2]
    product = conduction[:, :, None, :, None] * valence[:, None, :, None, :]
    return product.reshape(points, fine_bands * fine_bands, coarse_bands * coarse_bands)


def body(coarse_kernel, row_intersection, col_intersection, row_nearest, col_nearest, qp_energy):
    fine_pairs = NBF * NBF
    coarse_pairs = NBC * NBC
    row_coef = pair_coefficient(row_intersection).astype(jnp.bfloat16)
    local_rows = row_coef.shape[0] * fine_pairs
    selector = (row_nearest[:, None] == jnp.arange(RC, dtype=jnp.int32)[None, :]).astype(
        jnp.bfloat16
    )
    weights = (row_coef[:, :, None, :] * selector[:, None, :, None]).reshape(
        local_rows, RC * coarse_pairs
    )
    strip = jnp.dot(
        weights,
        lax.all_gather(coarse_kernel, "band", axis=0, tiled=True),
        preferred_element_type=jnp.float32,
    ).astype(jnp.bfloat16)
    held = strip.shape[1] // coarse_pairs
    strip_blocks = strip.reshape(local_rows, held, coarse_pairs)
    col_coef = pair_coefficient(col_intersection).astype(jnp.bfloat16)
    columns_here = col_nearest.shape[0]
    devices = lax.axis_size("kcol")
    capacity = max(2, (columns_here + devices - 1) // devices)
    holder = col_nearest // held
    local_slot = col_nearest % held
    hits = (holder[:, None] == jnp.arange(devices, dtype=jnp.int32)[None, :]).astype(jnp.int32)
    ranked = jnp.sum(jnp.cumsum(hits, axis=0) * hits, axis=1) - 1
    target = holder * capacity + ranked
    slot_hit = target[:, None] == jnp.arange(devices * capacity, dtype=jnp.int32)[None, :]
    request = (jnp.sum(jnp.where(slot_hit, local_slot[:, None] + 1, 0), axis=0) - 1).reshape(
        devices, capacity
    )
    picker = (
        lax.all_to_all(request, "kcol", split_axis=0, concat_axis=0, tiled=True)[..., None]
        == jnp.arange(held, dtype=jnp.int32)
    ).astype(jnp.bfloat16)
    chosen = jnp.einsum("smc,rcq->smrq", picker, strip_blocks, preferred_element_type=jnp.float32)
    returned = lax.all_to_all(
        chosen.astype(jnp.bfloat16), "kcol", split_axis=0, concat_axis=0, tiled=True
    )
    mine = jnp.take(returned.reshape(devices * capacity, local_rows, coarse_pairs), target, axis=0)
    expanded = jnp.einsum("jrq,jpq->rjp", mine, col_coef, preferred_element_type=jnp.float32)
    expanded = expanded.reshape(local_rows, columns_here * fine_pairs).astype(jnp.bfloat16)
    column_ids = lax.axis_index("kcol") * (columns_here * fine_pairs) + jnp.arange(
        columns_here * fine_pairs, dtype=jnp.int32
    )
    row_ids = lax.axis_index("band") * local_rows + jnp.arange(local_rows, dtype=jnp.int32)
    diagonal = jnp.where(row_ids[:, None] == column_ids[None, :], qp_energy[:, None], 0.0)
    return (expanded.astype(jnp.float32) + diagonal).astype(jnp.bfloat16)


def solution(mesh):
    return jax.shard_map(
        body,
        mesh=mesh,
        in_specs=(
            P("band", "kcol"),
            P(None, "band", None, None),
            P(None, "kcol", None, None),
            P("band"),
            P("kcol"),
            P("band"),
        ),
        out_specs=P("band", "kcol"),
        check_vma=False,
    )
```

profile of v0, /device:TPU:1, one launch (start us, length us, event | category | flops | bytes accessed | tf_op | source)
XLA Modules:
  0.0 458.6 jit_solution(5794267131194960956)
XLA Ops:
  0.0 0.7 and_select_fusion.1
  0.7 0.1 iota_compare_fusion.1
  0.8 0.1 fusion.6
  1.0 0.2 fusion.9
  1.2 0.1 select_reduce_fusion
  1.4 0.8 sub.19
  2.1 20.6 %all-to-all-start = ((s32[128,1,2]{2,1,0:T(1,128)}), s32[128,1,2]{2,1,0:T(1,128)S(1)}, u32[]{:S(2)}, u32[]{:S(2)}) async-start(s32[128,1,2]{2,1,0:T(1,128)} %bitcast.7), calls=%async_computation | async-start | bytes 131072 | tf_op jit(solution)/shard_map/all_to_all | solution.py:53
  22.7 0.7 slice_bitcast_fusion.3
  23.4 0.1 multiply_convert_fusion.1
  23.5 0.2 convert_element_type.56
  23.8 0.1 mul.93
  23.9 12.6 %all_gather.3 = bf16[576,576]{1,0:T(8,128)(2,1)S(1)} all-gather(bf16[144,576]{1,0:T(8,128)(2,1)} %param.6), channel_id=1, replica_groups=mesh['kcol'=128,'band'=4] {'band'}, dimensions={0}, use_global_device_ids=true | all-gather | bytes 829440 | tf_op jit(solution)/shard_map/all_gather | solution.py:34
  37.3 0.1 mul.94
  37.3 0.1 mul.95
  37.4 0.3 convolution_convert_fusion.1
  37.7 0.1 reshape.125
  37.8 0.0 all-to-all-done
  37.8 0.1 copy.26
  37.9 3.6 convolution_convert_fusion
  41.5 12.3 %copy.27 = bf16[128,2,64,144]{3,2,1,0:T(8,128)(2,1)} copy(bf16[128,2,64,144]{0,3,2,1:T(8,128)(2,1)} %convolution_convert_fusion) | data formatting | bytes 9437184 | tf_op jit(solution)/shard_map/convert_element_type | solution.py:58
  53.8 0.0 copy-start
  53.8 18.1 %all-to-all-start.1 = ((bf16[128,2,64,144]{3,2,1,0:T(8,128)(2,1)}), bf16[128,2,64,144]{3,2,1,0:T(8,128)(2,1)}, u32[]{:S(2)}, u32[]{:S(2)}) async-start(bf16[128,2,64,144]{3,2,1,0:T(8,128)(2,1)} %copy.27), calls=%async_computation.1 | async-start | bytes 16777216 | tf_op jit(solution)/shard_map/all_to_all | solution.py:57
  71.9 0.0 copy-done
  72.0 3.8 multiply_convert_fusion
  75.8 10.0 %copy.28 = bf16[144,64,144]{2,1,0:T(8,128)(2,1)} copy(bf16[144,64,144]{0,1,2:T(8,128)(2,1)} %bitcast.34) | data formatting | bytes 5308416 | tf_op jit(solution)/shard_map/convert_element_type | solution.py:39
  85.8 349.4 %all-to-all-done.1 = bf16[128,2,64,144]{3,2,1,0:T(8,128)(2,1)} async-done(((bf16[128,2,64,144]{3,2,1,0:T(8,128)(2,1)}), bf16[128,2,64,144]{3,2,1,0:T(8,128)(2,1)}, u32[]{:S(2)}, u32[]{:S(2)}) %all-to-all-start.1) | async-done | bytes 4718624 | tf_op jit(solution)/shard_map/all_to_all | solution.py:57
  435.1 10.9 %gather_fusion = bf16[144,64,144]{2,1,0:T(8,128)(2,1)} fusion(bf16[256,64,144]{2,1,0:T(8,128)(2,1)} %bitcast.14, s32[1024]{0:T(1024)S(1)} %pad_clamp_fusion), kind=kCustom, calls=%fused_computation | custom fusion | bytes 5308992 | tf_op jit(solution)/shard_map/jit(_take)/gather | solution.py:60
  446.1 7.4 %convert_convert_fusion = f32[144,64,64]{2,1,0:T(8,128)} fusion(bf16[144,64,144]{2,1,0:T(8,128)(2,1)} %copy.28, bf16[144,64,144]{2,1,0:T(8,128)(2,1)} %gather_fusion, pred[144]{0:T(512)(128)(4,1)S(1)} %get-tuple-element.5), kind=kOutput, calls=%fused_computation.7 | convolution fusion | flops 172376064 | bytes 7667856 | tf_op jit(solution)/shard_map/jrq,jpq->rjp/dot_general | solution.py:61
  453.4 0.0 copy-start.1
  453.4 3.8 copy.29
  457.2 0.0 copy-done.1
  457.2 1.4 add_convert_fusion
  (16 shorter events, 0.2 us)
Async XLA Ops:
  2.1 35.7 %all-to-all-start = ((s32[128,1,2]{2,1,0:T(1,128)}), s32[128,1,2]{2,1,0:T(1,128)S(1)}, u32[]{:S(2)}, u32[]{:S(2)}) async-start(s32[128,1,2]{2,1,0:T(1,128)} %bitcast.7), calls=%async_computation | async-start | bytes 131072 | tf_op jit(solution)/shard_map/all_to_all | solution.py:53
  53.8 18.1 %copy-start = (f32[2,144,8,12]{1,2,3,0:T(8,128)S(1)}, f32[2,144,8,12]{1,2,3,0:T(8,128)}, u32[]{:S(2)}) copy-start(f32[2,144,8,12]{1,2,3,0:T(8,128)} %param.8) | copy-start | bytes 331780
  53.8 381.3 %all-to-all-start.1 = ((bf16[128,2,64,144]{3,2,1,0:T(8,128)(2,1)}), bf16[128,2,64,144]{3,2,1,0:T(8,128)(2,1)}, u32[]{:S(2)}, u32[]{:S(2)}) async-start(bf16[128,2,64,144]{3,2,1,0:T(8,128)(2,1)} %copy.27), calls=%async_computation.1 | async-start | bytes 16777216 | tf_op jit(solution)/shard_map/all_to_all | solution.py:57
  453.4 3.8 copy-start.1
where the time goes:
time: 463 us; the launch traced here: 459 us
  waiting for transfers between devices  349 us (75%)
  local copies, waits for them, and re-layouts  39.3 us (8%)
  starting transfers between devices  38.6 us (8%)
  blocking collectives  12.6 us (3%)
  matrix products  11.2 us (2%)
  other arithmetic  6.61 us (1%)
    all_to_all x1, waiting for transfers between devices, body(): lax.all_to_all(chosen.astype(jnp.bfloat16), 'kcol', split_axis=0, concat_...  349 us
    all_to_all x1, starting transfers between devices, body(): lax.all_to_all(request, 'kcol', split_axis=0, concat_axis=0, tiled=True)  20.6 us
    all_to_all x1, starting transfers between devices, body(): lax.all_to_all(chosen.astype(jnp.bfloat16), 'kcol', split_axis=0, concat_...  18.1 us
    all_gather x1, blocking collectives, body(): lax.all_gather(coarse_kernel, 'band', axis=0, tiled=True)  12.6 us
    convert_element_type x1, local copies, waits for them, and re-layouts, body(): chosen.astype(jnp.bfloat16)  12.3 us
    gather x1, local copies, waits for them, and re-layouts, body(): jnp.take(returned.reshape(devices * capacity, local_rows, coarse_pairs),...  10.9 us
    convert_element_type x1, local copies, waits for them, and re-layouts, body(): col_coef = pair_coefficient(col_intersection).astype(jnp.bfloat16)  9.97 us
  transfers between devices with their start and end apart: 2, of which 1 were waited for; matrix products, arithmetic and copies ran while one was open for 3% of the time, Pallas kernels for 0%

commit v1 on v0

v1 whole, which is shorter than its diff:
```python
import jax
import jax.numpy as jnp
from jax import lax
from jax.experimental import pallas as pl
from jax.experimental.pallas import tpu as pltpu
from jax.sharding import Mesh
from jax.sharding import PartitionSpec as P

NBF = 8
NBC = 12
FP = NBF * NBF
CP = NBC * NBC
RC = 4
NY, NZ, NC, NB = 4, 16, 2, 4
GROUP = NY * NC
FC = 144
HELD = 4
CAP = 2
REL = (0, -1, 1, -2, -3, 2, 3, -4, -5, 4, 5, -6, -7, 6, 7, 8)
F32 = jnp.float32
BF16 = jnp.bfloat16


def iota(shape, dim):
    return lax.broadcasted_iota(jnp.int32, shape, dim)


def dot(a, b, dims=((1,), (0,))):
    return lax.dot_general(a, b, (dims, ((), ())), preferred_element_type=F32)


def whole(n):
    return [pl.BlockSpec(memory_space=pltpu.VMEM)] * n


def strip_kernel(pick_ref, k0, k1, k2, k3, coef_ref, out_ref):
    pick = pick_ref[0]
    rows = jnp.where(pick == 0, k0[...], k1[...])
    rows = jnp.where(pick == 2, k2[...], rows)
    rows = jnp.where(pick == 3, k3[...], rows)
    strip = dot(rows, coef_ref[...], ((0,), (1,))).astype(BF16)
    to = iota((CP, CP), 0)
    low = (to >> 3) * NBC + (to & 7)
    high = ((to - 96) >> 2) * NBC + 8 + (to & 3)
    order = (jnp.where(to < 96, low, high) == iota((CP, CP), 1)).astype(BF16)
    for pair in range(2):
        at = pair * 2 * CP
        both = jnp.concatenate([strip[at : at + CP], strip[at + CP : at + 2 * CP]], axis=1)
        out_ref[pair] = dot(order, both).astype(BF16)


def request_kernel(z_ref, row_ref, col_ref, conduction_ref, valence_ref, out_ref, slot_ref):
    z = z_ref[0]
    near = row_ref[...]
    holder = near >> 2
    earlier = ((col_ref[...] >> 2) == holder) & (iota((FC, FC), 0) < iota((FC, FC), 1))
    rank = jnp.sum(earlier.astype(jnp.int32), axis=0, keepdims=True)
    rel = ((holder >> 1) - z) & (NZ - 1)
    pos = jnp.zeros_like(rel)
    for k, offset in enumerate(REL):
        pos = jnp.where(rel == (offset % NZ), k, pos)
    group = (holder >> 5) * NC + (holder & 1)
    slot = (group * NZ + pos) * CAP + rank
    slot_ref[...] = slot
    lanes = 12 * 64
    source = iota((96, lanes), 0)
    lane = iota((96, lanes), 1)
    i, inner = lane >> 6, lane & 63
    spot = (inner & 7) * NBC + i
    table = jnp.zeros((FC, lanes), F32)
    for t, ref in enumerate((conduction_ref, valence_ref)):
        rest = ref[...]
        for s in range(3):
            term = rest.astype(BF16)
            rest = rest - term.astype(F32)
            place = ((source == spot) & ((inner >> 3) == s * 2 + t)).astype(BF16)
            table = table + dot(term, place)
    local = (col_ref[...] & 3).astype(F32)
    table = jnp.where((iota((FC, lanes), 1) & 63) == 48, local, table).astype(BF16)
    row = iota((GROUP * NZ, FC), 0) * CAP
    for r in range(CAP):
        one = (slot == row + r).astype(BF16)
        out_ref[:, r] = dot(one, table).astype(BF16).reshape(GROUP, NZ, lanes)


def expand_kernel(x_ref, u_ref, v_ref, local_ref):
    k = iota((256, 512), 0)
    n = iota((256, 512), 1)
    inner = k & 63
    want = jnp.where((n & 128) == 0, (n >> 3) & 7, n & 7)
    same = ((k >> 7) == ((n >> 6) & 1)) & (((k >> 6) & 1) == (n >> 8))
    same = same & (inner < 48) & (((inner >> 3) & 1) == ((n >> 7) & 1)) & ((inner & 7) == want)
    spread = same.astype(BF16)
    k = iota((256, 128), 0)
    n = iota((256, 128), 1)
    spread_local = (((k & 127) == 48) & ((k >> 7) == (n >> 6))).astype(BF16)
    for d in range(GROUP):
        lanes = pl.ds(d * 128, 128)
        for m in range(6):
            at = pl.ds(m * 128, 128)
            x = jnp.concatenate([x_ref[d, 0, :, at], x_ref[d, 1, :, at]], axis=1)
            y = dot(x, spread)
            for half in range(2):
                rows = pl.ds((m * 2 + half) * NZ, NZ)
                u_ref[d, rows] = y[:, half * 256 : half * 256 + 128]
                v_ref[d, rows] = y[:, half * 256 + 128 : half * 256 + 256]
            if m == 0:
                local_ref[:, lanes] = dot(x, spread_local)


def coefficients(u_ref, v_ref, d, pos):
    u = [jnp.broadcast_to(u_ref[d, pl.ds(i * NZ + pos, 1)], (8, 128)) for i in range(NBC)]
    v_low = v_ref[d, pl.ds(pos, 8, stride=NZ)]
    v_high = v_ref[d, pl.ds(8 * NZ + pos, 4, stride=NZ)]
    v_high = jnp.concatenate([v_high, v_high], axis=0)
    first = iota((8, 128), 0) < 4
    parts = [v_low * u[i] for i in range(NBC)]
    parts += [v_high * jnp.where(first, u[i], u[i + 1]) for i in range(0, NBC, 2)]
    return jnp.concatenate(parts, axis=0).astype(BF16)


def result_kernel(places, u_ref, v_ref, local_ref, *refs):
    strips, out_ref = refs[:-1], refs[-1]
    for at, (pos, pairs) in enumerate(places):
        blocks = [strips[a][b] for a, b in pairs]
        for chunk in range(4):
            lanes = pl.ds(chunk * 256, 256)
            coef = jnp.concatenate([coefficients(u_ref, v_ref, 2 * chunk + d, pos) for d in range(2)], axis=1)
            low = dot(blocks[0], coef, ((0,), (0,)))
            high = dot(blocks[1], coef, ((0,), (0,)))
            local = local_ref[pl.ds(pos, 1), lanes]
            res = jnp.where(local == 0, low[:FP], low[FP:])
            res = jnp.where(local == 2, high[:FP], res)
            res = jnp.where(local == 3, high[FP:], res).astype(BF16)
            for half in range(2):
                out_ref[chunk * 2 + half, at] = res[:, half * 128 : half * 128 + 128]


def assemble_kernel(slot_ref, where_ref, got_ref, qp_ref, out_ref):
    step = pl.program_id(0)
    tiles = out_ref.shape[1] // 128
    first = where_ref[0]
    lane = iota((FP, 128), 1)
    diagonal = jnp.where((lane & 63) == iota((FP, 128), 0), qp_ref[...], 0.0)
    for t in range(tiles):
        j = (step * tiles + t) * 2
        s0, s1 = slot_ref[j], slot_ref[j + 1]
        a = got_ref[s0 >> 1].astype(F32)
        b = got_ref[s1 >> 1].astype(F32)
        a = pltpu.roll(a, (s0 & 1) * 64, 1)
        b = pltpu.roll(b, (1 - (s1 & 1)) * 64, 1)
        tile = jnp.where(lane < FP, a, b)
        tile = tile + jnp.where(j + (lane >> 6) == first, diagonal, 0.0)
        out_ref[:, t * 128 : t * 128 + 128] = tile.astype(BF16)


def shift(x, axis, size, by):
    return lax.ppermute(x, axis, [(i, (i + by) % size) for i in range(size)])


def body(coarse_kernel, row_intersection, col_intersection, row_nearest, col_nearest, qp_energy):
    y, z, core, band = (lax.axis_index(a) for a in ("y", "z", "core", "band"))
    near = [coarse_kernel] + [shift(coarse_kernel, "band", NB, d) for d in range(1, NB)]
    pick = (band - row_nearest) % NB
    c, v = row_intersection[0, 0], row_intersection[1, 0]
    row_coef = (c[:, None, :, None] * v[None, :, None, :]).reshape(FP, CP).astype(BF16)

    smem = pl.BlockSpec(memory_space=pltpu.SMEM)
    limit = pltpu.CompilerParams(vmem_limit_bytes=48 * 2**20)
    request, slot = pl.pallas_call(
        request_kernel,
        in_specs=[smem] + whole(4),
        out_specs=whole(2),
        out_shape=[
            jax.ShapeDtypeStruct((GROUP, CAP, NZ, 768), BF16),
            jax.ShapeDtypeStruct((1, FC), jnp.int32),
        ],
        compiler_params=limit,
        name="request",
    )(
        z[None],
        col_nearest[None, :],
        col_nearest[:, None],
        col_intersection[0].reshape(FC, 96),
        col_intersection[1].reshape(FC, 96),
    )
    request = lax.all_to_all(request, ("y", "core"), 0, 0, tiled=True)
    lanes = GROUP * CAP * FP
    u, v, local = pl.pallas_call(
        expand_kernel,
        in_specs=whole(1),
        out_specs=whole(3),
        out_shape=[
            jax.ShapeDtypeStruct((GROUP, NBC * NZ, 128), F32),
            jax.ShapeDtypeStruct((GROUP, NBC * NZ, 128), F32),
            jax.ShapeDtypeStruct((NZ, lanes), F32),
        ],
        compiler_params=limit,
        name="expand",
    )(request)

    own = pl.pallas_call(
        strip_kernel,
        in_specs=[smem] + whole(5),
        out_specs=whole(1)[0],
        out_shape=jax.ShapeDtypeStruct((2, CP, 128), BF16),
        compiler_params=limit,
        name="strip",
    )(pick, *near, row_coef)

    chains = []
    for sign in (1, -1):
        one = shift(own, "z", NZ, sign)
        two = shift(jnp.concatenate([own, one]), "z", NZ, 2 * sign)
        four = shift(two, "z", NZ, 2 * sign)
        half = four[2:3] if sign == 1 else four[3:4]
        six = shift(jnp.concatenate([two[2:], four[:2], half]), "z", NZ, 3 * sign)
        chains.append((one, two, four, six))
    (p1, p2, p4, p6), (n1, n2, n4, n6) = chains
    strips = [own, p1, n1, p2, n2, p4, n4, p6, n6]
    places = [(0, ((0, 0), (0, 1))), (1, ((1, 0), (1, 1))), (2, ((2, 0), (2, 1)))]
    pos = 3
    for a in range(3, 9):
        for b in range(2):
            places.append((pos, ((a, 2 * b), (a, 2 * b + 1))))
            pos += 1
    places.append((15, ((7, 4), (8, 4))))

    def kernel(*refs):
        result_kernel(places, *refs)

    results = pl.pallas_call(
        kernel,
        in_specs=whole(3 + len(strips)),
        out_specs=whole(1)[0],
        out_shape=jax.ShapeDtypeStruct((GROUP, NZ, FP, 128), BF16),
        compiler_params=limit,
        name="result",
    )(u, v, local, *strips)
    got = lax.all_to_all(results, ("y", "core"), 0, 0, tiled=True)

    first = jnp.where((y == 0) & (z == 0) & (core == 0), band, -1)
    steps = 8
    columns = FC * FP
    return pl.pallas_call(
        assemble_kernel,
        grid=(steps,),
        in_specs=[
            smem,
            smem,
            pl.BlockSpec((GROUP * NZ, FP, 128), lambda i: (0, 0, 0)),
            pl.BlockSpec((FP, 1), lambda i: (0, 0)),
        ],
        out_specs=pl.BlockSpec((FP, columns // steps), lambda i: (0, i)),
        out_shape=jax.ShapeDtypeStruct((FP, columns), BF16),
        compiler_params=limit,
        name="assemble",
    )(slot.reshape(FC), first[None], got.reshape(GROUP * NZ, FP, 128), qp_energy[:, None])


def solution(mesh):
    fine = Mesh(mesh.devices.reshape(NY, NZ, NC, NB), ("y", "z", "core", "band"))
    kcol = ("y", "z", "core")
    return jax.shard_map(
        body,
        mesh=fine,
        in_specs=(
            P("band", kcol),
            P(None, "band", None, None),
            P(None, kcol, None, None),
            P("band"),
            P(kcol),
            P("band"),
        ),
        out_specs=P("band", kcol),
        check_vma=False,
    )
```

time: 463 us -> 123 us (0.27)
  the two profiles are of different devices: /device:TPU:1 before, /device:TPU:66 now
where the time goes in v1:
time: 123 us
  waiting for transfers between devices  54.5 us (44%)
  starting transfers between devices  52.7 us (43%)
  Pallas kernels  11.8 us (10%)
  local copies, waits for them, and re-layouts  2.38 us (2%)
    ppermute x11, starting transfers between devices, shift(): return lax.ppermute(x, axis, [(i, (i + by) % size) for i in range(size)])  43.7 us
    ppermute x11, waiting for transfers between devices, shift(): return lax.ppermute(x, axis, [(i, (i + by) % size) for i in range(size)])  27.4 us
    all_to_all x1, waiting for transfers between devices, body(): got = lax.all_to_all(results, ('y', 'core'), 0, 0, tiled=True)  27.1 us
    all_to_all x1, starting transfers between devices, body(): got = lax.all_to_all(results, ('y', 'core'), 0, 0, tiled=True)  4.58 us
    all_to_all x1, starting transfers between devices, body(): request = lax.all_to_all(request, ('y', 'core'), 0, 0, tiled=True)  4.47 us
    pallas_call x1, Pallas kernels, body(): pl.pallas_call(assemble_kernel, grid=(steps,), in_specs=[smem, smem, pl.B...  4.02 us
    pallas_call x1, Pallas kernels, body(): pl.pallas_call(kernel, in_specs=whole(3 + len(strips)), out_specs=whole(1...  3.76 us
  transfers between devices with their start and end apart: 13, of which 8 were waited for; matrix products, arithmetic and copies ran while one was open for 1% of the time, Pallas kernels for 3%

profile of v1, /device:TPU:66, one launch (start us, length us, event | category | flops | bytes accessed | tf_op | source)
XLA Modules:
  0.0 122.6 jit_solution(13037738009502148831)
XLA Ops:
  0.0 3.5 %collective-permute-start = (bf16[144,576]{1,0:T(8,128)(2,1)}, bf16[144,576]{1,0:T(8,128)(2,1)S(1)}, u32[]{:S(2)}, u32[]{:S(2)}) collective-permute-start(bf16[144,576]{1,0:T(8,128)(2,1)} %k0.1), channel_id=1, source_target_pairs={{0,1},{1,2},{2,3},{3,0},{4,5},{5,6},{6,7},{7,4},{8,9},{9,10},{10,1... | collective-permute-start | bytes 497672 | tf_op jit(solution)/shard_map/ppermute | solution.py:158
  3.5 3.0 %collective-permute-start.1 = (bf16[144,576]{1,0:T(8,128)(2,1)}, bf16[144,576]{1,0:T(8,128)(2,1)S(1)}, u32[]{:S(2)}, u32[]{:S(2)}) collective-permute-start(bf16[144,576]{1,0:T(8,128)(2,1)} %k0.1), channel_id=1, source_target_pairs={{0,2},{1,3},{2,0},{3,1},{4,6},{5,7},{6,4},{7,5},{8,10},{9,11},{10,... | collective-permute-start | bytes 497672 | tf_op jit(solution)/shard_map/ppermute | solution.py:158
  6.6 4.1 %collective-permute-start.2 = (bf16[144,576]{1,0:T(8,128)(2,1)}, bf16[144,576]{1,0:T(8,128)(2,1)S(1)}, u32[]{:S(2)}, u32[]{:S(2)}) collective-permute-start(bf16[144,576]{1,0:T(8,128)(2,1)} %k0.1), channel_id=1, source_target_pairs={{0,3},{1,0},{2,1},{3,2},{4,7},{5,4},{6,5},{7,6},{8,11},{9,8},{10,9... | collective-permute-start | bytes 497672 | tf_op jit(solution)/shard_map/ppermute | solution.py:158
  11.3 0.7 slice_bitcast_fusion.1
  12.0 0.1 multiply_convert_fusion
  12.1 0.2 convert_element_type.6.coef_ref
  12.4 2.3 %collective-permute-done.1.k2 = bf16[144,576]{1,0:T(8,128)(2,1)S(1)} collective-permute-done((bf16[144,576]{1,0:T(8,128)(2,1)}, bf16[144,576]{1,0:T(8,128)(2,1)S(1)}, u32[]{:S(2)}, u32[]{:S(2)}) %collective-permute-start.1) | collective-permute-done | bytes 165920 | tf_op jit(solution)/shard_map/ppermute | solution.py:158
  14.7 2.5 %collective-permute-done.2.k3 = bf16[144,576]{1,0:T(8,128)(2,1)S(1)} collective-permute-done((bf16[144,576]{1,0:T(8,128)(2,1)}, bf16[144,576]{1,0:T(8,128)(2,1)S(1)}, u32[]{:S(2)}, u32[]{:S(2)}) %collective-permute-start.2) | collective-permute-done | bytes 165920 | tf_op jit(solution)/shard_map/ppermute | solution.py:158
  17.2 0.9 copy-done
  18.1 0.5 strip.1.refs_3_
  18.7 3.8 %collective-permute-start.3 = (bf16[2,144,128]{2,1,0:T(8,128)(2,1)S(1)}, bf16[2,144,128]{2,1,0:T(8,128)(2,1)S(1)}, u32[]{:S(2)}, u32[]{:S(2)}) collective-permute-start(bf16[2,144,128]{2,1,0:T(8,128)(2,1)S(1)} %strip.1.refs_3_), channel_id=1, source_target_pairs={{0,8},{8,16},{16,24},{24,32},{32,40},{40,48},{48,56},{56,64},{64,7... | collective-permute-start | bytes 221192 | tf_op jit(solution)/shard_map/ppermute | solution.py:158
  22.5 2.0 %collective-permute-start.4 = (bf16[2,144,128]{2,1,0:T(8,128)(2,1)S(1)}, bf16[2,144,128]{2,1,0:T(8,128)(2,1)S(1)}, u32[]{:S(2)}, u32[]{:S(2)}) collective-permute-start(bf16[2,144,128]{2,1,0:T(8,128)(2,1)S(1)} %strip.1.refs_3_), channel_id=1, source_target_pairs={{0,120},{8,0},{16,8},{24,16},{32,24},{40,32},{48,40},{56,48},{64,5... | collective-permute-start | bytes 221192 | tf_op jit(solution)/shard_map/ppermute | solution.py:158
  24.5 0.4 collective-permute-done.3.refs_4_
  24.9 5.0 %collective-permute-done.4.refs_5_ = bf16[2,144,128]{2,1,0:T(8,128)(2,1)S(1)} collective-permute-done((bf16[2,144,128]{2,1,0:T(8,128)(2,1)S(1)}, bf16[2,144,128]{2,1,0:T(8,128)(2,1)S(1)}, u32[]{:S(2)}, u32[]{:S(2)}) %collective-permute-start.4) | collective-permute-done | bytes 73760 | tf_op jit(solution)/shard_map/ppermute | solution.py:158
  29.9 5.3 %collective-permute-start.5 = (bf16[4,144,128]{2,1,0:T(8,128)(2,1)S(1)}, bf16[4,144,128]{2,1,0:T(8,128)(2,1)S(1)}, u32[]{:S(2)}, u32[]{:S(2)}) collective-permute-start(bf16[4,144,128]{2,1,0:T(8,128)(2,1)S(1)} %get-tuple-element.18), channel_id=1, source_target_pairs={{0,16},{8,24},{16,32},{24,40},{32,48},{40,56},{48,64},{56,72},{64,... | collective-permute-start | bytes 442376 | tf_op jit(solution)/shard_map/ppermute | solution.py:158
  35.2 2.3 %collective-permute-start.6 = (bf16[4,144,128]{2,1,0:T(8,128)(2,1)S(1)}, bf16[4,144,128]{2,1,0:T(8,128)(2,1)S(1)}, u32[]{:S(2)}, u32[]{:S(2)}) collective-permute-start(bf16[4,144,128]{2,1,0:T(8,128)(2,1)S(1)} %get-tuple-element.17), channel_id=1, source_target_pairs={{0,112},{8,120},{16,0},{24,8},{32,16},{40,24},{48,32},{56,40},{64,... | collective-permute-start | bytes 442376 | tf_op jit(solution)/shard_map/ppermute | solution.py:158
  37.5 1.9 %collective-permute-done.5.refs_6_ = bf16[4,144,128]{2,1,0:T(8,128)(2,1)S(1)} collective-permute-done((bf16[4,144,128]{2,1,0:T(8,128)(2,1)S(1)}, bf16[4,144,128]{2,1,0:T(8,128)(2,1)S(1)}, u32[]{:S(2)}, u32[]{:S(2)}) %collective-permute-start.5) | collective-permute-done | bytes 147488 | tf_op jit(solution)/shard_map/ppermute | solution.py:158
  39.4 7.9 %collective-permute-start.7 = (bf16[4,144,128]{2,1,0:T(8,128)(2,1)S(1)}, bf16[4,144,128]{2,1,0:T(8,128)(2,1)S(1)}, u32[]{:S(2)}, u32[]{:S(2)}) collective-permute-start(bf16[4,144,128]{2,1,0:T(8,128)(2,1)S(1)} %collective-permute-done.5.refs_6_), channel_id=1, source_target_pairs={{0,16},{8,24},{16,32},{24,40},{32,48},{40,56},{48,64},{56,72},{64,... | collective-permute-start | bytes 442376 | tf_op jit(solution)/shard_map/ppermute | solution.py:158
  47.4 1.9 %collective-permute-start.8 = (bf16[4,144,128]{2,1,0:T(8,128)(2,1)S(1)}, bf16[4,144,128]{2,1,0:T(8,128)(2,1)S(1)}, u32[]{:S(2)}, u32[]{:S(2)}) collective-permute-start(bf16[4,144,128]{2,1,0:T(8,128)(2,1)S(1)} %collective-permute-done.6.refs_7_), channel_id=1, source_target_pairs={{0,112},{8,120},{16,0},{24,8},{32,16},{40,24},{48,32},{56,40},{64,... | collective-permute-start | bytes 442376 | tf_op jit(solution)/shard_map/ppermute | solution.py:158
  49.3 0.1 copy.12.col_ref
  49.8 1.6 %request.1 = (bf16[8,2,16,768]{3,2,1,0:T(8,128)(2,1)}, s32[1,144]{1,0:T(1,128)S(1)}) custom-call(s32[1]{0:T(128)} %bitcast.z_ref, s32[1,144]{1,0:T(1,128)S(1)} %bitcast.18, s32[144,1]{1,0:T(8,128)S(1)} %copy.12.col_ref, f32[144,96]{1,0:T(8,128)S(1)} %copy.13.conduction_ref, f32[144,96]{1,0:T(8,128)S(1)} %copy.14.valence_ref), custom_call_target="tpu_custom_call" | custom-call | tf_op jit(solution)/shard_map/request/pallas_call | solution.py:170
  51.4 4.5 %all-to-all-start = ((bf16[8,2,16,768]{3,2,1,0:T(8,128)(2,1)}), bf16[8,2,16,768]{3,2,1,0:T(8,128)(2,1)S(1)}, u32[]{:S(2)}, u32[]{:S(2)}) async-start(bf16[8,2,16,768]{3,2,1,0:T(8,128)(2,1)} %get-tuple-element.11), calls=%async_computation | async-start | bytes 786432 | tf_op jit(solution)/shard_map/all_to_all | solution.py:187
  56.0 7.8 %collective-permute-start.9 = (bf16[5,144,128]{2,1,0:T(8,128)(2,1)S(1)}, bf16[5,144,128]{2,1,0:T(8,128)(2,1)S(1)}, u32[]{:S(2)}, u32[]{:S(2)}) collective-permute-start(bf16[5,144,128]{2,1,0:T(8,128)(2,1)S(1)} %pad_maximum_fusion), channel_id=1, source_target_pairs={{0,24},{8,32},{16,40},{24,48},{32,56},{40,64},{48,72},{56,80},{64,... | collective-permute-start | bytes 552968 | tf_op jit(solution)/shard_map/ppermute | solution.py:158
  63.9 1.9 %collective-permute-start.10 = (bf16[5,144,128]{2,1,0:T(8,128)(2,1)S(1)}, bf16[5,144,128]{2,1,0:T(8,128)(2,1)S(1)}, u32[]{:S(2)}, u32[]{:S(2)}) collective-permute-start(bf16[5,144,128]{2,1,0:T(8,128)(2,1)S(1)} %pad_maximum_fusion.1), channel_id=1, source_target_pairs={{0,104},{8,112},{16,120},{24,0},{32,8},{40,16},{48,24},{56,32},{64... | collective-permute-start | bytes 552968 | tf_op jit(solution)/shard_map/ppermute | solution.py:158
  65.8 1.9 %expand.1 = (f32[8,192,128]{2,1,0:T(8,128)S(1)}, f32[8,192,128]{2,1,0:T(8,128)S(1)}, f32[16,1024]{1,0:T(8,128)S(1)}) custom-call(bf16[8,2,16,768]{3,2,1,0:T(8,128)(2,1)S(1)} %all-to-all-done.x_ref), custom_call_target="tpu_custom_call" | custom-call | tf_op jit(solution)/shard_map/expand/pallas_call | solution.py:189
  67.7 8.1 %collective-permute-done.9.refs_10_ = bf16[5,144,128]{2,1,0:T(8,128)(2,1)S(1)} collective-permute-done((bf16[5,144,128]{2,1,0:T(8,128)(2,1)S(1)}, bf16[5,144,128]{2,1,0:T(8,128)(2,1)S(1)}, u32[]{:S(2)}, u32[]{:S(2)}) %collective-permute-start.9) | collective-permute-done | bytes 184352 | tf_op jit(solution)/shard_map/ppermute | solution.py:158
  75.8 7.2 %collective-permute-done.10.refs_11_ = bf16[5,144,128]{2,1,0:T(8,128)(2,1)S(1)} collective-permute-done((bf16[5,144,128]{2,1,0:T(8,128)(2,1)S(1)}, bf16[5,144,128]{2,1,0:T(8,128)(2,1)S(1)}, u32[]{:S(2)}, u32[]{:S(2)}) %collective-permute-start.10) | collective-permute-done | bytes 184352 | tf_op jit(solution)/shard_map/ppermute | solution.py:158
  83.0 3.8 %result.1 = bf16[8,16,64,128]{3,2,1,0:T(8,128)(2,1)} custom-call(f32[8,192,128]{2,1,0:T(8,128)S(1)} %get-tuple-element.12.refs_0_, f32[8,192,128]{2,1,0:T(8,128)S(1)} %get-tuple-element.13.refs_1_, f32[16,1024]{1,0:T(8,128)S(1)} %get-tuple-element.14.refs_2_, bf16[2,144,128]{2,1,0:T(8,128)(2,1)S(1)} %strip.1.refs_3_, ...), custom_call_target="tpu_custom_call" | custom-call | tf_op jit(solution)/shard_map/result/pallas_call | solution.py:232
  86.8 4.6 %all-to-all-start.1 = ((bf16[8,16,64,128]{3,2,1,0:T(8,128)(2,1)}), bf16[8,16,64,128]{3,2,1,0:T(8,128)(2,1)S(1)}, u32[]{:S(2)}, u32[]{:S(2)}) async-start(bf16[8,16,64,128]{3,2,1,0:T(8,128)(2,1)} %result.1), calls=%async_computation.1 | async-start | bytes 4194304 | tf_op jit(solution)/shard_map/all_to_all | solution.py:240
  91.4 0.1 copy.15.qp_ref
  91.5 27.1 %all-to-all-done.1 = bf16[8,16,64,128]{3,2,1,0:T(8,128)(2,1)S(1)} async-done(((bf16[8,16,64,128]{3,2,1,0:T(8,128)(2,1)}), bf16[8,16,64,128]{3,2,1,0:T(8,128)(2,1)S(1)}, u32[]{:S(2)}, u32[]{:S(2)}) %all-to-all-start.1) | async-done | bytes 2097184 | tf_op jit(solution)/shard_map/all_to_all | solution.py:240
  118.6 4.0 %assemble.1 = bf16[64,9216]{1,0:T(8,128)(2,1)} custom-call(s32[144]{0:T(256)S(1)} %bitcast.19, s32[1]{0:T(128)} %bitcast.4.where_ref, bf16[128,64,128]{2,1,0:T(8,128)(2,1)S(1)} %bitcast.16, f32[64,1]{1,0:T(8,128)S(1)} %copy.15.qp_ref), custom_call_target="tpu_custom_call" | custom-call | tf_op jit(solution)/shard_map/assemble/pallas_call | solution.py:245
  (27 shorter events, 0.4 us)
Async XLA Ops:
  0.0 49.3 %copy-start.2 = (f32[2,144,8,12]{1,2,3,0:T(8,128)S(1)}, f32[2,144,8,12]{1,2,3,0:T(8,128)}, u32[]{:S(2)}) copy-start(f32[2,144,8,12]{1,2,3,0:T(8,128)} %param.8) | copy-start | bytes 331780
  0.0 49.3 %copy-start.1 = (s32[144]{0:T(256)S(1)}, s32[144]{0:T(256)}, u32[]{:S(2)}) copy-start(s32[144]{0:T(256)} %param.10) | copy-start | bytes 1732
  0.0 12.3 %collective-permute-start = (bf16[144,576]{1,0:T(8,128)(2,1)}, bf16[144,576]{1,0:T(8,128)(2,1)S(1)}, u32[]{:S(2)}, u32[]{:S(2)}) collective-permute-start(bf16[144,576]{1,0:T(8,128)(2,1)} %k0.1), channel_id=1, source_target_pairs={{0,1},{1,2},{2,3},{3,0},{4,5},{5,6},{6,7},{7,4},{8,9},{9,10},{10,1... | collective-permute-start | bytes 497672 | tf_op jit(solution)/shard_map/ppermute | solution.py:158
  3.5 11.2 %collective-permute-start.1 = (bf16[144,576]{1,0:T(8,128)(2,1)}, bf16[144,576]{1,0:T(8,128)(2,1)S(1)}, u32[]{:S(2)}, u32[]{:S(2)}) collective-permute-start(bf16[144,576]{1,0:T(8,128)(2,1)} %k0.1), channel_id=1, source_target_pairs={{0,2},{1,3},{2,0},{3,1},{4,6},{5,7},{6,4},{7,5},{8,10},{9,11},{10,... | collective-permute-start | bytes 497672 | tf_op jit(solution)/shard_map/ppermute | solution.py:158
  6.6 10.6 %collective-permute-start.2 = (bf16[144,576]{1,0:T(8,128)(2,1)}, bf16[144,576]{1,0:T(8,128)(2,1)S(1)}, u32[]{:S(2)}, u32[]{:S(2)}) collective-permute-start(bf16[144,576]{1,0:T(8,128)(2,1)} %k0.1), channel_id=1, source_target_pairs={{0,3},{1,0},{2,1},{3,2},{4,7},{5,4},{6,5},{7,6},{8,11},{9,8},{10,9... | collective-permute-start | bytes 497672 | tf_op jit(solution)/shard_map/ppermute | solution.py:158
  17.2 0.9 copy-start
  18.7 6.2 %collective-permute-start.3 = (bf16[2,144,128]{2,1,0:T(8,128)(2,1)S(1)}, bf16[2,144,128]{2,1,0:T(8,128)(2,1)S(1)}, u32[]{:S(2)}, u32[]{:S(2)}) collective-permute-start(bf16[2,144,128]{2,1,0:T(8,128)(2,1)S(1)} %strip.1.refs_3_), channel_id=1, source_target_pairs={{0,8},{8,16},{16,24},{24,32},{32,40},{40,48},{48,56},{56,64},{64,7... | collective-permute-start | bytes 221192 | tf_op jit(solution)/shard_map/ppermute | solution.py:158
  22.5 7.4 %collective-permute-start.4 = (bf16[2,144,128]{2,1,0:T(8,128)(2,1)S(1)}, bf16[2,144,128]{2,1,0:T(8,128)(2,1)S(1)}, u32[]{:S(2)}, u32[]{:S(2)}) collective-permute-start(bf16[2,144,128]{2,1,0:T(8,128)(2,1)S(1)} %strip.1.refs_3_), channel_id=1, source_target_pairs={{0,120},{8,0},{16,8},{24,16},{32,24},{40,32},{48,40},{56,48},{64,5... | collective-permute-start | bytes 221192 | tf_op jit(solution)/shard_map/ppermute | solution.py:158
  29.9 9.5 %collective-permute-start.5 = (bf16[4,144,128]{2,1,0:T(8,128)(2,1)S(1)}, bf16[4,144,128]{2,1,0:T(8,128)(2,1)S(1)}, u32[]{:S(2)}, u32[]{:S(2)}) collective-permute-start(bf16[4,144,128]{2,1,0:T(8,128)(2,1)S(1)} %get-tuple-element.18), channel_id=1, source_target_pairs={{0,16},{8,24},{16,32},{24,40},{32,48},{40,56},{48,64},{56,72},{64,... | collective-permute-start | bytes 442376 | tf_op jit(solution)/shard_map/ppermute | solution.py:158
  35.2 12.2 %collective-permute-start.6 = (bf16[4,144,128]{2,1,0:T(8,128)(2,1)S(1)}, bf16[4,144,128]{2,1,0:T(8,128)(2,1)S(1)}, u32[]{:S(2)}, u32[]{:S(2)}) collective-permute-start(bf16[4,144,128]{2,1,0:T(8,128)(2,1)S(1)} %get-tuple-element.17), channel_id=1, source_target_pairs={{0,112},{8,120},{16,0},{24,8},{32,16},{40,24},{48,32},{56,40},{64,... | collective-permute-start | bytes 442376 | tf_op jit(solution)/shard_map/ppermute | solution.py:158
  39.4 16.5 %collective-permute-start.7 = (bf16[4,144,128]{2,1,0:T(8,128)(2,1)S(1)}, bf16[4,144,128]{2,1,0:T(8,128)(2,1)S(1)}, u32[]{:S(2)}, u32[]{:S(2)}) collective-permute-start(bf16[4,144,128]{2,1,0:T(8,128)(2,1)S(1)} %collective-permute-done.5.refs_6_), channel_id=1, source_target_pairs={{0,16},{8,24},{16,32},{24,40},{32,48},{40,56},{48,64},{56,72},{64,... | collective-permute-start | bytes 442376 | tf_op jit(solution)/shard_map/ppermute | solution.py:158
  47.4 16.5 %collective-permute-start.8 = (bf16[4,144,128]{2,1,0:T(8,128)(2,1)S(1)}, bf16[4,144,128]{2,1,0:T(8,128)(2,1)S(1)}, u32[]{:S(2)}, u32[]{:S(2)}) collective-permute-start(bf16[4,144,128]{2,1,0:T(8,128)(2,1)S(1)} %collective-permute-done.6.refs_7_), channel_id=1, source_target_pairs={{0,112},{8,120},{16,0},{24,8},{32,16},{40,24},{48,32},{56,40},{64,... | collective-permute-start | bytes 442376 | tf_op jit(solution)/shard_map/ppermute | solution.py:158
  51.4 14.4 %all-to-all-start = ((bf16[8,2,16,768]{3,2,1,0:T(8,128)(2,1)}), bf16[8,2,16,768]{3,2,1,0:T(8,128)(2,1)S(1)}, u32[]{:S(2)}, u32[]{:S(2)}) async-start(bf16[8,2,16,768]{3,2,1,0:T(8,128)(2,1)} %get-tuple-element.11), calls=%async_computation | async-start | bytes 786432 | tf_op jit(solution)/shard_map/all_to_all | solution.py:187
  56.0 19.9 %collective-permute-start.9 = (bf16[5,144,128]{2,1,0:T(8,128)(2,1)S(1)}, bf16[5,144,128]{2,1,0:T(8,128)(2,1)S(1)}, u32[]{:S(2)}, u32[]{:S(2)}) collective-permute-start(bf16[5,144,128]{2,1,0:T(8,128)(2,1)S(1)} %pad_maximum_fusion), channel_id=1, source_target_pairs={{0,24},{8,32},{16,40},{24,48},{32,56},{40,64},{48,72},{56,80},{64,... | collective-permute-start | bytes 552968 | tf_op jit(solution)/shard_map/ppermute | solution.py:158
  63.9 19.1 %collective-permute-start.10 = (bf16[5,144,128]{2,1,0:T(8,128)(2,1)S(1)}, bf16[5,144,128]{2,1,0:T(8,128)(2,1)S(1)}, u32[]{:S(2)}, u32[]{:S(2)}) collective-permute-start(bf16[5,144,128]{2,1,0:T(8,128)(2,1)S(1)} %pad_maximum_fusion.1), channel_id=1, source_target_pairs={{0,104},{8,112},{16,120},{24,0},{32,8},{40,16},{48,24},{56,32},{64... | collective-permute-start | bytes 552968 | tf_op jit(solution)/shard_map/ppermute | solution.py:158
  86.8 4.6 %copy-start.3 = (f32[64]{0:T(128)S(1)}, f32[64]{0:T(128)}, u32[]{:S(2)}) copy-start(f32[64]{0:T(128)} %param.11) | copy-start | bytes 772
  86.8 31.8 %all-to-all-start.1 = ((bf16[8,16,64,128]{3,2,1,0:T(8,128)(2,1)}), bf16[8,16,64,128]{3,2,1,0:T(8,128)(2,1)S(1)}, u32[]{:S(2)}, u32[]{:S(2)}) async-start(bf16[8,16,64,128]{3,2,1,0:T(8,128)(2,1)} %result.1), calls=%async_computation.1 | async-start | bytes 4194304 | tf_op jit(solution)/shard_map/all_to_all | solution.py:240

commit v2 on v1

v2 whole, which is shorter than its diff:
```python
import functools

import jax
import jax.numpy as jnp
from jax import lax
from jax.experimental import pallas as pl
from jax.experimental.pallas import tpu as pltpu
from jax.sharding import Mesh
from jax.sharding import PartitionSpec as P

NBF = 8
NBC = 12
FP = NBF * NBF
CP = NBC * NBC
RC = 4
NY, NZ, NC, NB = 4, 16, 2, 4
GROUP = NY * NC
FC = 144
HELD = 4
CAP = 2
PARTS = ((0, 5), (5, 11), (11, 16))
HALF = NZ // 2
COSTS = (10, 20, 4)
F32 = jnp.float32
BF16 = jnp.bfloat16


def iota(shape, dim):
    return lax.broadcasted_iota(jnp.int32, shape, dim)


def dot(a, b, dims=((1,), (0,))):
    return lax.dot_general(a, b, (dims, ((), ())), preferred_element_type=F32)


def whole(n):
    return [pl.BlockSpec(memory_space=pltpu.VMEM)] * n


def strip_kernel(pick_ref, k0, k1, k2, k3, coef_ref, out_ref):
    pick = pick_ref[0]
    rows = jnp.where(pick == 0, k0[...], k1[...])
    rows = jnp.where(pick == 2, k2[...], rows)
    rows = jnp.where(pick == 3, k3[...], rows)
    strip = dot(rows, coef_ref[...], ((0,), (1,))).astype(BF16)
    to = iota((CP, CP), 0)
    low = (to >> 3) * NBC + (to & 7)
    high = ((to - 96) >> 2) * NBC + 8 + (to & 3)
    order = (jnp.where(to < 96, low, high) == iota((CP, CP), 1)).astype(BF16)
    for pair in range(2):
        at = pair * 2 * CP
        both = jnp.concatenate([strip[at : at + CP], strip[at + CP : at + 2 * CP]], axis=1)
        out_ref[pair] = dot(order, both).astype(BF16)


def request_kernel(z_ref, row_ref, conduction_ref, valence_ref, out_ref, block_ref):
    z = z_ref[0]
    near = row_ref[...]
    holder = near >> 2
    square = (FC, FC)
    here = iota(square, 0) == iota(square, 1)
    column = jnp.sum(jnp.where(here, near, 0), axis=1, keepdims=True)
    earlier = ((column >> 2) == holder) & (iota(square, 0) < iota(square, 1))
    rank = jnp.sum(earlier.astype(jnp.int32), axis=0, keepdims=True)
    rel = ((holder >> 1) - z) & (NZ - 1)
    far = jnp.minimum(rel, NZ - rel)
    core = holder & 1
    server = jnp.where((far & 7) == 0, core, (rel < 8).astype(jnp.int32))
    pos = jnp.where((far & 7) == 0, (far >> 3) * 15, 2 * far - 1 + (core ^ server))
    group = (holder >> 5) * NC + server
    slot = (group * NZ + pos) * CAP + rank
    block = jnp.zeros_like(pos)
    for lo, hi in PARTS:
        block = jnp.where((pos >= lo) & (pos < hi), lo * GROUP + group * (hi - lo) + pos - lo, block)
    block_ref[...] = block * CAP + rank
    lanes = 12 * 64
    source = iota((96, lanes), 0)
    lane = iota((96, lanes), 1)
    i, inner = lane >> 6, lane & 63
    spot = (inner & 7) * NBC + i
    table = jnp.zeros((FC, lanes), F32)
    for t, ref in enumerate((conduction_ref, valence_ref)):
        rest = ref[...]
        for s in range(3):
            term = rest.astype(BF16)
            rest = rest - term.astype(F32)
            place = ((source == spot) & ((inner >> 3) == s * 2 + t)).astype(BF16)
            table = table + dot(term, place)
    local = (column & 3).astype(F32)
    table = jnp.where((iota((FC, lanes), 1) & 63) == 48, local, table).astype(BF16)
    row = iota((GROUP * NZ, FC), 0) * CAP
    for r in range(CAP):
        one = (slot == row + r).astype(BF16)
        out_ref[:, r] = dot(one, table).astype(BF16).reshape(GROUP, NZ, lanes)


def expand_kernel(x_ref, u0_ref, v0_ref, u1_ref, v1_ref, local_ref):
    k = iota((256, 512), 0)
    n = iota((256, 512), 1)
    inner = k & 63
    want = jnp.where((n & 128) == 0, (n >> 3) & 7, n & 7)
    same = ((k >> 7) == ((n >> 6) & 1)) & (((k >> 6) & 1) == (n >> 8))
    same = same & (inner < 48) & (((inner >> 3) & 1) == ((n >> 7) & 1)) & ((inner & 7) == want)
    spread = same.astype(BF16)
    k = iota((256, 128), 0)
    n = iota((256, 128), 1)
    spread_local = (((k & 127) == 48) & ((k >> 7) == (n >> 6))).astype(BF16)
    for d in range(GROUP):
        lanes = pl.ds(d * 128, 128)
        for m in range(6):
            at = pl.ds(m * 128, 128)
            x = jnp.concatenate([x_ref[d, 0, :, at], x_ref[d, 1, :, at]], axis=1)
            y = dot(x, spread)
            for half in range(2):
                rows = pl.ds((m * 2 + half) * HALF, HALF)
                for n, (u_ref, v_ref) in enumerate(((u0_ref, v0_ref), (u1_ref, v1_ref))):
                    part = y[n * HALF : (n + 1) * HALF, half * 256 : half * 256 + 256]
                    u_ref[d, rows] = part[:, :128]
                    v_ref[d, rows] = part[:, 128:]
            if m == 0:
                local_ref[:, lanes] = dot(x, spread_local)


def coefficients(u_ref, v_ref, d, pos):
    u = [jnp.broadcast_to(u_ref[d, pl.ds(i * HALF + pos, 1)], (8, 128)) for i in range(NBC)]
    v_low = v_ref[d, pl.ds(pos, 8, stride=HALF)]
    v_high = v_ref[d, pl.ds(8 * HALF + pos, 4, stride=HALF)]
    v_high = jnp.concatenate([v_high, v_high], axis=0)
    first = iota((8, 128), 0) < 4
    parts = [v_low * u[i] for i in range(NBC)]
    parts += [v_high * jnp.where(first, u[i], u[i + 1]) for i in range(0, NBC, 2)]
    return jnp.concatenate(parts, axis=0).astype(BF16)


def result_kernel(places, halves, local_ref, *refs):
    factors = {h: refs[2 * n : 2 * n + 2] for n, h in enumerate(halves)}
    strips, out_ref = refs[2 * len(halves) : -1], refs[-1]
    for at, (pos, pairs) in enumerate(places):
        blocks = [strips[a][b] for a, b in pairs]
        u_ref, v_ref = factors[pos // HALF]
        for chunk in range(4):
            lanes = pl.ds(chunk * 256, 256)
            coef = jnp.concatenate([coefficients(u_ref, v_ref, 2 * chunk + d, pos % HALF) for d in range(2)], axis=1)
            low = dot(blocks[0], coef, ((0,), (0,)))
            high = dot(blocks[1], coef, ((0,), (0,)))
            local = local_ref[pl.ds(pos, 1), lanes]
            res = jnp.where(local == 0, low[:FP], low[FP:])
            res = jnp.where(local == 2, high[:FP], res)
            res = jnp.where(local == 3, high[FP:], res).astype(BF16)
            for half in range(2):
                out_ref[chunk * 2 + half, at] = res[:, half * 128 : half * 128 + 128]


def assemble_kernel(block_ref, where_ref, *refs):
    parts, (qp_ref, out_ref, got_ref, sems) = refs[: len(PARTS)], refs[len(PARTS) :]
    step = pl.program_id(0)

    @pl.when(step == 0)
    def _():
        copies = []
        for n, (lo, hi) in enumerate(PARTS):
            at = pl.ds(lo * GROUP, (hi - lo) * GROUP)
            copies.append(pltpu.make_async_copy(parts[n], got_ref.at[at], sems.at[n]))
            copies[-1].start()
        for copy in copies:
            copy.wait()

    tiles = out_ref.shape[1] // 128
    first = where_ref[0]
    lane = iota((FP, 128), 1)
    diagonal = jnp.where((lane & 63) == iota((FP, 128), 0), qp_ref[...], 0.0)
    for t in range(tiles):
        j = (step * tiles + t) * 2
        s0, s1 = block_ref[j], block_ref[j + 1]
        a = got_ref[s0 >> 1].astype(F32)
        b = got_ref[s1 >> 1].astype(F32)
        a = pltpu.roll(a, (s0 & 1) * 64, 1)
        b = pltpu.roll(b, (1 - (s1 & 1)) * 64, 1)
        out_ref[:, t * 128 : t * 128 + 128] = jnp.where(lane < FP, a, b).astype(BF16)

    @pl.when((step == 0) & (first >= 0))
    def _():
        for t in range(2):
            at = slice(t * 128, t * 128 + 128)
            add = jnp.where(2 * t + (lane >> 6) == first, diagonal, 0.0)
            out_ref[:, at] = (out_ref[:, at].astype(F32) + add).astype(BF16)


def shift(x, axis, size, by):
    return lax.ppermute(x, axis, [(i, (i + by) % size) for i in range(size)])


def along(x, by):
    pairs = [(z * NC + c, (z + (by if c == 0 else -by)) % NZ * NC + c) for z in range(NZ) for c in range(NC)]
    return lax.ppermute(x, ("z", "core"), pairs)


def body(coarse_kernel, row_intersection, col_intersection, row_nearest, col_nearest, qp_energy):
    y, z, core, band = (lax.axis_index(a) for a in ("y", "z", "core", "band"))
    near = [coarse_kernel] + [shift(coarse_kernel, "band", NB, d) for d in range(1, NB)]
    pick = (band - row_nearest) % NB
    c, v = row_intersection[0, 0], row_intersection[1, 0]
    row_coef = (c[:, None, :, None] * v[None, :, None, :]).reshape(FP, CP).astype(BF16)

    smem = pl.BlockSpec(memory_space=pltpu.SMEM)
    limit = pltpu.CompilerParams(vmem_limit_bytes=16 * 2**20)
    request, block = pl.pallas_call(
        request_kernel,
        in_specs=[smem] + whole(3),
        out_specs=whole(2),
        out_shape=[
            jax.ShapeDtypeStruct((GROUP, CAP, NZ, 768), BF16),
            jax.ShapeDtypeStruct((1, FC), jnp.int32),
        ],
        compiler_params=limit,
        name="request",
    )(
        z[None],
        col_nearest[None, :],
        col_intersection[0].reshape(FC, 96),
        col_intersection[1].reshape(FC, 96),
    )
    request, *near = lax.optimization_barrier((request, *near))
    request = lax.all_to_all(request, ("y", "core"), 0, 0, tiled=True)
    lanes = GROUP * CAP * FP
    *factors, local = pl.pallas_call(
        expand_kernel,
        in_specs=whole(1),
        out_specs=whole(5),
        out_shape=[
            *[jax.ShapeDtypeStruct((GROUP, NBC * HALF, 128), F32)] * 4,
            jax.ShapeDtypeStruct((NZ, lanes), F32),
        ],
        compiler_params=limit,
        name="expand",
    )(request)

    own = pl.pallas_call(
        strip_kernel,
        in_specs=[smem] + whole(5),
        out_specs=whole(1)[0],
        out_shape=jax.ShapeDtypeStruct((2, CP, 128), BF16),
        compiler_params=limit,
        name="strip",
    )(pick, *near, row_coef)

    own = jnp.concatenate([own, shift(own, "core", NC, 1)])
    one = along(own, 1)
    two = along(jnp.concatenate([own, one]), 2)
    four = along(two, 2)
    six = along(four, 2)
    eight = along(six[4:6], 1)
    strips = [own, one, two, four, six, eight]
    places = [(0, ((0, 0), (0, 1)))]
    for a, blocks in ((1, 2), (2, 4), (3, 4), (4, 4), (5, 1)):
        places += [(len(places) + b, ((a, 2 * b), (a, 2 * b + 1))) for b in range(blocks)]

    got = []
    for lo, hi in PARTS:
        used = sorted({a for _, pairs in places[lo:hi] for a, _ in pairs})
        halves = sorted({pos // HALF for pos in range(lo, hi)})
        mine = [(pos, tuple((used.index(a), b) for a, b in pairs)) for pos, pairs in places[lo:hi]]
        if got:
            local, last = lax.optimization_barrier((local, last))
        results = pl.pallas_call(
            functools.partial(result_kernel, mine, halves),
            in_specs=whole(1 + 2 * len(halves) + len(used)),
            out_specs=whole(1)[0],
            out_shape=jax.ShapeDtypeStruct((GROUP, hi - lo, FP, 128), BF16),
            compiler_params=limit,
            cost_estimate=pl.CostEstimate(flops=COSTS[len(got)] * 10**9, bytes_accessed=10**6, transcendentals=0),
            name="result",
        )(local, *[f for h in halves for f in factors[2 * h : 2 * h + 2]], *[strips[a] for a in used])
        last = results
        if got:
            results, got[-1] = lax.optimization_barrier((results, got[-1]))
        got.append(lax.all_to_all(results, ("y", "core"), 0, 0, tiled=True).reshape(-1, FP, 128))

    first = jnp.where((y == 0) & (z == 0) & (core == 0), band, -1)
    steps = 4
    columns = FC * FP
    return pl.pallas_call(
        assemble_kernel,
        grid=(steps,),
        in_specs=[
            smem,
            smem,
            *[pl.BlockSpec(memory_space=pl.ANY)] * len(got),
            pl.BlockSpec((FP, 1), lambda i: (0, 0)),
        ],
        out_specs=pl.BlockSpec((FP, columns // steps), lambda i: (0, i)),
        out_shape=jax.ShapeDtypeStruct((FP, columns), BF16),
        scratch_shapes=[pltpu.VMEM((GROUP * NZ, FP, 128), BF16), pltpu.SemaphoreType.DMA((len(got),))],
        compiler_params=limit,
        name="assemble",
    )(block.reshape(FC), first[None], *got, qp_energy[:, None])


def solution(mesh):
    fine = Mesh(mesh.devices.reshape(NY, NZ, NC, NB), ("y", "z", "core", "band"))
    kcol = ("y", "z", "core")
    return jax.shard_map(
        body,
        mesh=fine,
        in_specs=(
            P("band", kcol),
            P(None, "band", None, None),
            P(None, kcol, None, None),
            P("band"),
            P(kcol),
            P("band"),
        ),
        out_specs=P("band", kcol),
        check_vma=False,
    )
```

time: 123 us -> 105 us (0.85)
  the two profiles are of different devices: /device:TPU:66 before, /device:TPU:1 now
where the time goes in v2:
time: 105 us; the launch traced here: 104 us
  starting transfers between devices  61.6 us (59%)
  waiting for transfers between devices  25.4 us (24%)
  Pallas kernels  13.6 us (13%)
  local copies, waits for them, and re-layouts  2.56 us (2%)
    ppermute x5, starting transfers between devices, along(): return lax.ppermute(x, ('z', 'core'), pairs)  25.3 us
    ppermute x4, starting transfers between devices, shift(): return lax.ppermute(x, axis, [(i, (i + by) % size) for i in range(size)])  18.5 us
    all_to_all x3, waiting for transfers between devices, body(): lax.all_to_all(results, ('y', 'core'), 0, 0, tiled=True)  16.5 us
    all_to_all x3, starting transfers between devices, body(): lax.all_to_all(results, ('y', 'core'), 0, 0, tiled=True)  13.2 us
    pallas_call x3, Pallas kernels, body(): pl.pallas_call(functools.partial(result_kernel, mine, halves), in_specs=w...  6.4 us
    all_to_all x1, starting transfers between devices, body(): request = lax.all_to_all(request, ('y', 'core'), 0, 0, tiled=True)  4.59 us
    all_to_all x1, waiting for transfers between devices, body(): request = lax.all_to_all(request, ('y', 'core'), 0, 0, tiled=True)  4.42 us
    ppermute x5, waiting for transfers between devices, along(): return lax.ppermute(x, ('z', 'core'), pairs)  3.62 us
  transfers between devices with their start and end apart: 13, of which 8 were waited for; matrix products, arithmetic and copies ran while one was open for 2% of the time, Pallas kernels for 9%

profile of v2, /device:TPU:1, one launch (start us, length us, event | category | flops | bytes accessed | tf_op | source)
XLA Modules:
  0.0 104.2 jit_solution(8922354692937897413)
XLA Ops:
  0.0 4.1 %collective-permute-start = (bf16[144,576]{1,0:T(8,128)(2,1)}, bf16[144,576]{1,0:T(8,128)(2,1)S(1)}, u32[]{:S(2)}, u32[]{:S(2)}) collective-permute-start(bf16[144,576]{1,0:T(8,128)(2,1)} %k0), channel_id=1, source_target_pairs={{0,1},{1,2},{2,3},{3,0},{4,5},{5,6},{6,7},{7,4},{8,9},{9,10},{10,1... | collective-permute-start | bytes 497672 | tf_op jit(solution)/shard_map/ppermute | solution.py:190
  4.1 4.4 %collective-permute-start.1 = (bf16[144,576]{1,0:T(8,128)(2,1)}, bf16[144,576]{1,0:T(8,128)(2,1)S(1)}, u32[]{:S(2)}, u32[]{:S(2)}) collective-permute-start(bf16[144,576]{1,0:T(8,128)(2,1)} %k0), channel_id=1, source_target_pairs={{0,2},{1,3},{2,0},{3,1},{4,6},{5,7},{6,4},{7,5},{8,10},{9,11},{10,... | collective-permute-start | bytes 497672 | tf_op jit(solution)/shard_map/ppermute | solution.py:190
  8.4 3.1 %collective-permute-start.2 = (bf16[144,576]{1,0:T(8,128)(2,1)}, bf16[144,576]{1,0:T(8,128)(2,1)S(1)}, u32[]{:S(2)}, u32[]{:S(2)}) collective-permute-start(bf16[144,576]{1,0:T(8,128)(2,1)} %k0), channel_id=1, source_target_pairs={{0,3},{1,0},{2,1},{3,2},{4,7},{5,4},{6,5},{7,6},{8,11},{9,8},{10,9... | collective-permute-start | bytes 497672 | tf_op jit(solution)/shard_map/ppermute | solution.py:190
  12.2 1.0 fusion
  13.5 0.1 multiply_convert_fusion
  13.6 0.2 convert_element_type.6.coef_ref
  13.9 1.6 %request.1 = (bf16[8,2,16,768]{3,2,1,0:T(8,128)(2,1)}, s32[1,144]{1,0:T(1,128)S(1)}) custom-call(s32[1]{0:T(128)} %bitcast.z_ref, s32[1,144]{1,0:T(1,128)S(1)} %bitcast.20, f32[144,96]{1,0:T(8,128)S(1)} %copy.12.conduction_ref, f32[144,96]{1,0:T(8,128)S(1)} %copy.13.valence_ref), custom_call_target="tpu_custom_call" | custom-call | tf_op jit(solution)/shard_map/request/pallas_call | solution.py:207
  15.5 0.5 strip.1
  16.1 7.0 %collective-permute-start.3 = (bf16[2,144,128]{2,1,0:T(8,128)(2,1)S(1)}, bf16[2,144,128]{2,1,0:T(8,128)(2,1)S(1)}, u32[]{:S(2)}, u32[]{:S(2)}) collective-permute-start(bf16[2,144,128]{2,1,0:T(8,128)(2,1)S(1)} %strip.1), channel_id=1, source_target_pairs={{0,4},{4,0},{1,5},{5,1},{2,6},{6,2},{3,7},{7,3},{8,12},{12,8},{9,1... | collective-permute-start | bytes 221192 | tf_op jit(solution)/shard_map/ppermute | solution.py:190
  23.1 0.9 collective-permute-done.3
  24.0 8.3 %collective-permute-start.4 = (bf16[4,144,128]{2,1,0:T(8,128)(2,1)S(1)}, bf16[4,144,128]{2,1,0:T(8,128)(2,1)S(1)}, u32[]{:S(2)}, u32[]{:S(2)}) collective-permute-start(bf16[4,144,128]{2,1,0:T(8,128)(2,1)S(1)} %pad_maximum_fusion.1.refs_2_), channel_id=1, source_target_pairs={{0,8},{4,124},{8,16},{12,4},{16,24},{20,12},{24,32},{28,20},{32,40... | collective-permute-start | bytes 442376 | tf_op jit(solution)/shard_map/ppermute | solution.py:195
  32.3 4.6 %all-to-all-start = ((bf16[8,2,16,768]{3,2,1,0:T(8,128)(2,1)}), bf16[8,2,16,768]{3,2,1,0:T(8,128)(2,1)S(1)}, u32[]{:S(2)}, u32[]{:S(2)}) async-start(bf16[8,2,16,768]{3,2,1,0:T(8,128)(2,1)} %get-tuple-element.25), calls=%async_computation | async-start | bytes 786432 | tf_op jit(solution)/shard_map/all_to_all | solution.py:224
  36.9 3.6 %collective-permute-start.5 = (bf16[8,144,128]{2,1,0:T(8,128)(2,1)S(1)}, bf16[8,144,128]{2,1,0:T(8,128)(2,1)S(1)}, u32[]{:S(2)}, u32[]{:S(2)}) collective-permute-start(bf16[8,144,128]{2,1,0:T(8,128)(2,1)S(1)} %pad_maximum_fusion), channel_id=1, source_target_pairs={{0,16},{4,116},{8,24},{12,124},{16,32},{20,4},{24,40},{28,12},{32,... | collective-permute-start | bytes 884744 | tf_op jit(solution)/shard_map/ppermute | solution.py:195
  40.5 4.4 %all-to-all-done.x_ref = bf16[8,2,16,768]{3,2,1,0:T(8,128)(2,1)S(1)} async-done(((bf16[8,2,16,768]{3,2,1,0:T(8,128)(2,1)}), bf16[8,2,16,768]{3,2,1,0:T(8,128)(2,1)S(1)}, u32[]{:S(2)}, u32[]{:S(2)}) %all-to-all-start) | async-done | bytes 393248 | tf_op jit(solution)/shard_map/all_to_all | solution.py:224
  44.9 1.9 %expand.1 = (f32[8,96,128]{2,1,0:T(8,128)S(1)}, f32[8,96,128]{2,1,0:T(8,128)S(1)}, f32[8,96,128]{2,1,0:T(8,128)S(1)}, f32[8,96,128]{2,1,0:T(8,128)S(1)}, f32[16,1024]{1,0:T(8,128)S(1)}) custom-call(bf16[8,2,16,768]{3,2,1,0:T(8,128)(2,1)S(1)} %all-to-all-done.x_ref), custom_call_target="tpu_custom_call" | custom-call | tf_op jit(solution)/shard_map/expand/pallas_call | solution.py:226
  46.8 0.2 collective-permute-done.5.refs_4_
  47.0 5.0 %collective-permute-start.6 = (bf16[8,144,128]{2,1,0:T(8,128)(2,1)S(1)}, bf16[8,144,128]{2,1,0:T(8,128)(2,1)}, u32[]{:S(2)}, u32[]{:S(2)}) collective-permute-start(bf16[8,144,128]{2,1,0:T(8,128)(2,1)S(1)} %collective-permute-done.5.refs_4_), channel_id=1, source_target_pairs={{0,16},{4,116},{8,24},{12,124},{16,32},{20,4},{24,40},{28,12},{32,... | collective-permute-start | bytes 884744 | tf_op jit(solution)/shard_map/ppermute | solution.py:195
  52.0 1.8 %result.3 = bf16[8,5,64,128]{3,2,1,0:T(8,128)(2,1)} custom-call(f32[16,1024]{1,0:T(8,128)S(1)} %get-tuple-element.37.local_ref, f32[8,96,128]{2,1,0:T(8,128)S(1)} %get-tuple-element.27.refs_0_, f32[8,96,128]{2,1,0:T(8,128)S(1)} %get-tuple-element.28.refs_1_, bf16[4,144,128]{2,1,0:T(8,128)(2,1)S(1)} %pad_maximum_fusion.1.refs_2_, ...), custom_call_target="tpu_custom_call" | custom-call | flops 10000000000 | bytes 1000000 | tf_op jit(solution)/shard_map/result/pallas_call | solution.py:265
  53.7 4.6 %all-to-all-start.1 = ((bf16[8,5,64,128]{3,2,1,0:T(8,128)(2,1)}), bf16[8,5,64,128]{3,2,1,0:T(8,128)(2,1)S(1)}, u32[]{:S(2)}, u32[]{:S(2)}) async-start(bf16[8,5,64,128]{3,2,1,0:T(8,128)(2,1)} %result.3), calls=%async_computation.1 | async-start | bytes 1310720 | tf_op jit(solution)/shard_map/all_to_all | solution.py:277
  58.3 0.5 collective-permute-done.6.refs_5_
  58.8 6.0 %collective-permute-start.7 = (bf16[8,144,128]{2,1,0:T(8,128)(2,1)}, bf16[8,144,128]{2,1,0:T(8,128)(2,1)S(1)}, u32[]{:S(2)}, u32[]{:S(2)}) collective-permute-start(bf16[8,144,128]{2,1,0:T(8,128)(2,1)} %collective-permute-done.6.refs_5_), channel_id=1, source_target_pairs={{0,16},{4,116},{8,24},{12,124},{16,32},{20,4},{24,40},{28,12},{32,... | collective-permute-start | bytes 884744 | tf_op jit(solution)/shard_map/ppermute | solution.py:195
  64.8 1.0 copy-done.3
  65.7 2.9 %result.4 = bf16[8,6,64,128]{3,2,1,0:T(8,128)(2,1)} custom-call(f32[16,1024]{1,0:T(8,128)S(1)} %get-tuple-element.37.local_ref, f32[8,96,128]{2,1,0:T(8,128)S(1)} %get-tuple-element.27.refs_0_, f32[8,96,128]{2,1,0:T(8,128)S(1)} %get-tuple-element.28.refs_1_, f32[8,96,128]{2,1,0:T(8,128)S(1)} %get-tuple-element.34.refs_2_.refs_0_, ...), custom_call_target="tpu_custom_call" | custom-call | flops 20000000000 | bytes 1000000 | tf_op jit(solution)/shard_map/result/pallas_call | solution.py:265
  68.6 0.5 all-to-all-done.1
  69.2 4.3 %all-to-all-start.2 = ((bf16[8,6,64,128]{3,2,1,0:T(8,128)(2,1)}), bf16[8,6,64,128]{3,2,1,0:T(8,128)(2,1)S(1)}, u32[]{:S(2)}, u32[]{:S(2)}) async-start(bf16[8,6,64,128]{3,2,1,0:T(8,128)(2,1)} %result.4), calls=%async_computation.2 | async-start | bytes 1572864 | tf_op jit(solution)/shard_map/all_to_all | solution.py:277
  73.5 2.5 %collective-permute-start.8 = (bf16[2,144,128]{2,1,0:T(8,128)(2,1)S(1)}, bf16[2,144,128]{2,1,0:T(8,128)(2,1)S(1)}, u32[]{:S(2)}, u32[]{:S(2)}) collective-permute-start(bf16[2,144,128]{2,1,0:T(8,128)(2,1)S(1)} %slice.20), channel_id=1, source_target_pairs={{0,8},{4,124},{8,16},{12,4},{16,24},{20,12},{24,32},{28,20},{32,40... | collective-permute-start | bytes 221192 | tf_op jit(solution)/shard_map/ppermute | solution.py:195
  76.0 3.0 %collective-permute-done.8.refs_3_ = bf16[2,144,128]{2,1,0:T(8,128)(2,1)S(1)} collective-permute-done((bf16[2,144,128]{2,1,0:T(8,128)(2,1)S(1)}, bf16[2,144,128]{2,1,0:T(8,128)(2,1)S(1)}, u32[]{:S(2)}, u32[]{:S(2)}) %collective-permute-start.8) | collective-permute-done | bytes 73760 | tf_op jit(solution)/shard_map/ppermute | solution.py:195
  79.0 1.7 %result.5 = bf16[8,5,64,128]{3,2,1,0:T(8,128)(2,1)} custom-call(f32[16,1024]{1,0:T(8,128)S(1)} %get-tuple-element.37.local_ref, f32[8,96,128]{2,1,0:T(8,128)S(1)} %get-tuple-element.34.refs_2_.refs_0_, f32[8,96,128]{2,1,0:T(8,128)S(1)} %get-tuple-element.35.refs_3_.refs_1_, bf16[8,144,128]{2,1,0:T(8,128)(2,1)S(1)} %collective-permute-done.7.refs_2_, ...), custom_call_target="tpu_custom_call" | custom-call | flops 4000000000 | bytes 1000000 | tf_op jit(solution)/shard_map/result/pallas_call | solution.py:265
  80.7 5.1 %all-to-all-done.2 = bf16[8,6,64,128]{3,2,1,0:T(8,128)(2,1)S(1)} async-done(((bf16[8,6,64,128]{3,2,1,0:T(8,128)(2,1)}), bf16[8,6,64,128]{3,2,1,0:T(8,128)(2,1)S(1)}, u32[]{:S(2)}, u32[]{:S(2)}) %all-to-all-start.2) | async-done | bytes 786464 | tf_op jit(solution)/shard_map/all_to_all | solution.py:277
  85.8 4.3 %all-to-all-start.3 = ((bf16[8,5,64,128]{3,2,1,0:T(8,128)(2,1)}), bf16[8,5,64,128]{3,2,1,0:T(8,128)(2,1)S(1)}, u32[]{:S(2)}, u32[]{:S(2)}) async-start(bf16[8,5,64,128]{3,2,1,0:T(8,128)(2,1)} %result.5), calls=%async_computation.3 | async-start | bytes 1310720 | tf_op jit(solution)/shard_map/all_to_all | solution.py:277
  90.2 10.8 %all-to-all-done.3 = bf16[8,5,64,128]{3,2,1,0:T(8,128)(2,1)S(1)} async-done(((bf16[8,5,64,128]{3,2,1,0:T(8,128)(2,1)}), bf16[8,5,64,128]{3,2,1,0:T(8,128)(2,1)S(1)}, u32[]{:S(2)}, u32[]{:S(2)}) %all-to-all-start.3) | async-done | bytes 655392 | tf_op jit(solution)/shard_map/all_to_all | solution.py:277
  101.0 3.2 %assemble.1 = bf16[64,9216]{1,0:T(8,128)(2,1)} custom-call(s32[144]{0:T(256)S(1)} %bitcast.21, s32[1]{0:T(128)} %bitcast.3.where_ref, bf16[40,64,128]{2,1,0:T(8,128)(2,1)S(1)} %bitcast.18, bf16[48,64,128]{2,1,0:T(8,128)(2,1)S(1)} %bitcast.17, bf16[40,64,128]{2,1,0:T(8,128)(2,1)S(1)} %bitcast.19, f32[64,1]{1,0:T(8,128)S(1)} %copy.14.refs_3_), custom_call_target="tpu_custom_call" | custom-call | tf_op jit(solution)/shard_map/assemble/pallas_call | solution.py:282
  (27 shorter events, 0.5 us)
Async XLA Ops:
  0.0 13.5 %copy-start.4 = (f32[2,1,8,12]{3,2,1,0:T(8,128)S(1)}, f32[2,1,8,12]{3,2,1,0:T(8,128)}, u32[]{:S(2)}) copy-start(f32[2,1,8,12]{3,2,1,0:T(8,128)} %param.7) | copy-start | bytes 2308
  0.0 13.9 %copy-start.1 = (s32[144]{0:T(256)S(1)}, s32[144]{0:T(256)}, u32[]{:S(2)}) copy-start(s32[144]{0:T(256)} %param.10) | copy-start | bytes 1732
  0.0 15.5 %collective-permute-start = (bf16[144,576]{1,0:T(8,128)(2,1)}, bf16[144,576]{1,0:T(8,128)(2,1)S(1)}, u32[]{:S(2)}, u32[]{:S(2)}) collective-permute-start(bf16[144,576]{1,0:T(8,128)(2,1)} %k0), channel_id=1, source_target_pairs={{0,1},{1,2},{2,3},{3,0},{4,5},{5,6},{6,7},{7,4},{8,9},{9,10},{10,1... | collective-permute-start | bytes 497672 | tf_op jit(solution)/shard_map/ppermute | solution.py:190
  4.1 11.4 %collective-permute-start.1 = (bf16[144,576]{1,0:T(8,128)(2,1)}, bf16[144,576]{1,0:T(8,128)(2,1)S(1)}, u32[]{:S(2)}, u32[]{:S(2)}) collective-permute-start(bf16[144,576]{1,0:T(8,128)(2,1)} %k0), channel_id=1, source_target_pairs={{0,2},{1,3},{2,0},{3,1},{4,6},{5,7},{6,4},{7,5},{8,10},{9,11},{10,... | collective-permute-start | bytes 497672 | tf_op jit(solution)/shard_map/ppermute | solution.py:190
  8.4 7.1 %collective-permute-start.2 = (bf16[144,576]{1,0:T(8,128)(2,1)}, bf16[144,576]{1,0:T(8,128)(2,1)S(1)}, u32[]{:S(2)}, u32[]{:S(2)}) collective-permute-start(bf16[144,576]{1,0:T(8,128)(2,1)} %k0), channel_id=1, source_target_pairs={{0,3},{1,0},{2,1},{3,2},{4,7},{5,4},{6,5},{7,6},{8,11},{9,8},{10,9... | collective-permute-start | bytes 497672 | tf_op jit(solution)/shard_map/ppermute | solution.py:190
  12.2 3.4 %copy-start = (bf16[144,576]{1,0:T(8,128)(2,1)S(1)}, bf16[144,576]{1,0:T(8,128)(2,1)}, u32[]{:S(2)}) copy-start(bf16[144,576]{1,0:T(8,128)(2,1)} %k0) | copy-start | bytes 497668
  16.1 7.9 %collective-permute-start.3 = (bf16[2,144,128]{2,1,0:T(8,128)(2,1)S(1)}, bf16[2,144,128]{2,1,0:T(8,128)(2,1)S(1)}, u32[]{:S(2)}, u32[]{:S(2)}) collective-permute-start(bf16[2,144,128]{2,1,0:T(8,128)(2,1)S(1)} %strip.1), channel_id=1, source_target_pairs={{0,4},{4,0},{1,5},{5,1},{2,6},{6,2},{3,7},{7,3},{8,12},{12,8},{9,1... | collective-permute-start | bytes 221192 | tf_op jit(solution)/shard_map/ppermute | solution.py:190
  24.0 12.9 %collective-permute-start.4 = (bf16[4,144,128]{2,1,0:T(8,128)(2,1)S(1)}, bf16[4,144,128]{2,1,0:T(8,128)(2,1)S(1)}, u32[]{:S(2)}, u32[]{:S(2)}) collective-permute-start(bf16[4,144,128]{2,1,0:T(8,128)(2,1)S(1)} %pad_maximum_fusion.1.refs_2_), channel_id=1, source_target_pairs={{0,8},{4,124},{8,16},{12,4},{16,24},{20,12},{24,32},{28,20},{32,40... | collective-permute-start | bytes 442376 | tf_op jit(solution)/shard_map/ppermute | solution.py:195
  32.3 12.7 %all-to-all-start = ((bf16[8,2,16,768]{3,2,1,0:T(8,128)(2,1)}), bf16[8,2,16,768]{3,2,1,0:T(8,128)(2,1)S(1)}, u32[]{:S(2)}, u32[]{:S(2)}) async-start(bf16[8,2,16,768]{3,2,1,0:T(8,128)(2,1)} %get-tuple-element.25), calls=%async_computation | async-start | bytes 786432 | tf_op jit(solution)/shard_map/all_to_all | solution.py:224
  36.9 10.1 %collective-permute-start.5 = (bf16[8,144,128]{2,1,0:T(8,128)(2,1)S(1)}, bf16[8,144,128]{2,1,0:T(8,128)(2,1)S(1)}, u32[]{:S(2)}, u32[]{:S(2)}) collective-permute-start(bf16[8,144,128]{2,1,0:T(8,128)(2,1)S(1)} %pad_maximum_fusion), channel_id=1, source_target_pairs={{0,16},{4,116},{8,24},{12,124},{16,32},{20,4},{24,40},{28,12},{32,... | collective-permute-start | bytes 884744 | tf_op jit(solution)/shard_map/ppermute | solution.py:195
  47.0 6.7 %copy-start.2 = (bf16[8,144,128]{2,1,0:T(8,128)(2,1)}, bf16[8,144,128]{2,1,0:T(8,128)(2,1)S(1)}, u32[]{:S(2)}) copy-start(bf16[8,144,128]{2,1,0:T(8,128)(2,1)S(1)} %collective-permute-done.5.refs_4_) | copy-start | bytes 884740
  47.0 11.8 %collective-permute-start.6 = (bf16[8,144,128]{2,1,0:T(8,128)(2,1)S(1)}, bf16[8,144,128]{2,1,0:T(8,128)(2,1)}, u32[]{:S(2)}, u32[]{:S(2)}) collective-permute-start(bf16[8,144,128]{2,1,0:T(8,128)(2,1)S(1)} %collective-permute-done.5.refs_4_), channel_id=1, source_target_pairs={{0,16},{4,116},{8,24},{12,124},{16,32},{20,4},{24,40},{28,12},{32,... | collective-permute-start | bytes 884744 | tf_op jit(solution)/shard_map/ppermute | solution.py:195
  53.7 15.4 %all-to-all-start.1 = ((bf16[8,5,64,128]{3,2,1,0:T(8,128)(2,1)}), bf16[8,5,64,128]{3,2,1,0:T(8,128)(2,1)S(1)}, u32[]{:S(2)}, u32[]{:S(2)}) async-start(bf16[8,5,64,128]{3,2,1,0:T(8,128)(2,1)} %result.3), calls=%async_computation.1 | async-start | bytes 1310720 | tf_op jit(solution)/shard_map/all_to_all | solution.py:277
  58.8 14.7 %collective-permute-start.7 = (bf16[8,144,128]{2,1,0:T(8,128)(2,1)}, bf16[8,144,128]{2,1,0:T(8,128)(2,1)S(1)}, u32[]{:S(2)}, u32[]{:S(2)}) collective-permute-start(bf16[8,144,128]{2,1,0:T(8,128)(2,1)} %collective-permute-done.6.refs_5_), channel_id=1, source_target_pairs={{0,16},{4,116},{8,24},{12,124},{16,32},{20,4},{24,40},{28,12},{32,... | collective-permute-start | bytes 884744 | tf_op jit(solution)/shard_map/ppermute | solution.py:195
  64.8 1.0 copy-start.3
  69.2 16.6 %all-to-all-start.2 = ((bf16[8,6,64,128]{3,2,1,0:T(8,128)(2,1)}), bf16[8,6,64,128]{3,2,1,0:T(8,128)(2,1)S(1)}, u32[]{:S(2)}, u32[]{:S(2)}) async-start(bf16[8,6,64,128]{3,2,1,0:T(8,128)(2,1)} %result.4), calls=%async_computation.2 | async-start | bytes 1572864 | tf_op jit(solution)/shard_map/all_to_all | solution.py:277
  73.5 5.4 %collective-permute-start.8 = (bf16[2,144,128]{2,1,0:T(8,128)(2,1)S(1)}, bf16[2,144,128]{2,1,0:T(8,128)(2,1)S(1)}, u32[]{:S(2)}, u32[]{:S(2)}) collective-permute-start(bf16[2,144,128]{2,1,0:T(8,128)(2,1)S(1)} %slice.20), channel_id=1, source_target_pairs={{0,8},{4,124},{8,16},{12,4},{16,24},{20,12},{24,32},{28,20},{32,40... | collective-permute-start | bytes 221192 | tf_op jit(solution)/shard_map/ppermute | solution.py:195
  80.7 9.4 %copy-start.5 = (f32[64]{0:T(128)S(1)}, f32[64]{0:T(128)}, u32[]{:S(2)}) copy-start(f32[64]{0:T(128)} %param.11) | copy-start | bytes 772
  85.8 15.2 %all-to-all-start.3 = ((bf16[8,5,64,128]{3,2,1,0:T(8,128)(2,1)}), bf16[8,5,64,128]{3,2,1,0:T(8,128)(2,1)S(1)}, u32[]{:S(2)}, u32[]{:S(2)}) async-start(bf16[8,5,64,128]{3,2,1,0:T(8,128)(2,1)} %result.5), calls=%async_computation.3 | async-start | bytes 1310720 | tf_op jit(solution)/shard_map/all_to_all | solution.py:277

commit v3 on v2

--- a/solution.py
+++ b/solution.py
@@ -18,9 +18,10 @@
 FC = 144
 HELD = 4
 CAP = 2
-PARTS = ((0, 5), (5, 11), (11, 16))
+PARTS = ((0, 6), (6, 11), (11, 16))
+RANGES = (((0, 3), (3, 6)), ((6, 11),), ((11, 16),))
 HALF = NZ // 2
-COSTS = (10, 20, 4)
+COSTS = {0: 0, 3: 10, 6: 20, 11: 4}
 F32 = jnp.float32
 BF16 = jnp.bfloat16
 
@@ -37,7 +38,7 @@
     return [pl.BlockSpec(memory_space=pltpu.VMEM)] * n
 
 
-def strip_kernel(pick_ref, k0, k1, k2, k3, coef_ref, out_ref):
+def strip_kernel(pick_ref, k0, k2, k1, k3, coef_ref, out_ref):
     pick = pick_ref[0]
     rows = jnp.where(pick == 0, k0[...], k1[...])
     rows = jnp.where(pick == 2, k2[...], rows)
@@ -132,9 +133,10 @@
     return jnp.concatenate(parts, axis=0).astype(BF16)
 
 
-def result_kernel(places, halves, local_ref, *refs):
+def result_kernel(places, halves, offset, local_ref, *refs):
     factors = {h: refs[2 * n : 2 * n + 2] for n, h in enumerate(halves)}
-    strips, out_ref = refs[2 * len(halves) : -1], refs[-1]
+    strips, (out_ref, kept_ref, sems) = refs[2 * len(halves) : -3], refs[-3:]
+    copies = []
     for at, (pos, pairs) in enumerate(places):
         blocks = [strips[a][b] for a, b in pairs]
         u_ref, v_ref = factors[pos // HALF]
@@ -148,42 +150,48 @@
             res = jnp.where(local == 2, high[:FP], res)
             res = jnp.where(local == 3, high[FP:], res).astype(BF16)
             for half in range(2):
-                out_ref[chunk * 2 + half, at] = res[:, half * 128 : half * 128 + 128]
+                kept_ref[at, chunk * 2 + half] = res[:, half * 128 : half * 128 + 128]
+        copies.append(pltpu.make_async_copy(kept_ref.at[at], out_ref.at[:, offset + at], sems.at[at]))
+        copies[-1].start()
+    for copy in copies:
+        copy.wait()
 
 
 def assemble_kernel(block_ref, where_ref, *refs):
-    parts, (qp_ref, out_ref, got_ref, sems) = refs[: len(PARTS)], refs[len(PARTS) :]
-    step = pl.program_id(0)
-
-    @pl.when(step == 0)
-    def _():
-        copies = []
-        for n, (lo, hi) in enumerate(PARTS):
-            at = pl.ds(lo * GROUP, (hi - lo) * GROUP)
-            copies.append(pltpu.make_async_copy(parts[n], got_ref.at[at], sems.at[n]))
-            copies[-1].start()
-        for copy in copies:
-            copy.wait()
-
-    tiles = out_ref.shape[1] // 128
+    parts, (qp_ref, out_ref, got_ref, full_ref, in_sems, out_sems) = refs[: len(PARTS)], refs[len(PARTS) :]
+    copies = []
+    for n, (lo, hi) in enumerate(PARTS):
+        at = pl.ds(lo * GROUP, (hi - lo) * GROUP)
+        copies.append(pltpu.make_async_copy(parts[n], got_ref.at[at], in_sems.at[n]))
+        copies[-1].start()
+    for copy in copies:
+        copy.wait()
     first = where_ref[0]
     lane = iota((FP, 128), 1)
-    diagonal = jnp.where((lane & 63) == iota((FP, 128), 0), qp_ref[...], 0.0)
-    for t in range(tiles):
-        j = (step * tiles + t) * 2
-        s0, s1 = block_ref[j], block_ref[j + 1]
-        a = got_ref[s0 >> 1].astype(F32)
-        b = got_ref[s1 >> 1].astype(F32)
-        a = pltpu.roll(a, (s0 & 1) * 64, 1)
-        b = pltpu.roll(b, (1 - (s1 & 1)) * 64, 1)
-        out_ref[:, t * 128 : t * 128 + 128] = jnp.where(lane < FP, a, b).astype(BF16)
-
-    @pl.when((step == 0) & (first >= 0))
-    def _():
-        for t in range(2):
-            at = slice(t * 128, t * 128 + 128)
-            add = jnp.where(2 * t + (lane >> 6) == first, diagonal, 0.0)
-            out_ref[:, at] = (out_ref[:, at].astype(F32) + add).astype(BF16)
+    tiles = FC // 2
+    chunks = out_sems.shape[0]
+    copies = []
+    for chunk in range(chunks):
+        for t in range(chunk * tiles // chunks, (chunk + 1) * tiles // chunks):
+            s0, s1 = block_ref[2 * t], block_ref[2 * t + 1]
+            a = pltpu.roll(got_ref[s0 >> 1], (s0 & 1) * 64, 1)
+            b = pltpu.roll(got_ref[s1 >> 1], (1 - (s1 & 1)) * 64, 1)
+            full_ref[:, t * 128 : t * 128 + 128] = jnp.where(lane < FP, a, b)
+        if chunk == 0:
+
+            @pl.when(first >= 0)
+            def _():
+                diagonal = jnp.where((lane & 63) == iota((FP, 128), 0), qp_ref[...], 0.0)
+                for t in range(2):
+                    at = slice(t * 128, t * 128 + 128)
+                    add = jnp.where(2 * t + (lane >> 6) == first, diagonal, 0.0)
+                    full_ref[:, at] = (full_ref[:, at].astype(F32) + add).astype(BF16)
+
+        at = pl.ds(chunk * tiles // chunks * 128, tiles // chunks * 128)
+        copies.append(pltpu.make_async_copy(full_ref.at[:, at], out_ref.at[:, at], out_sems.at[chunk]))
+        copies[-1].start()
+    for copy in copies:
+        copy.wait()
 
 
 def shift(x, axis, size, by):
@@ -197,7 +205,7 @@
 
 def body(coarse_kernel, row_intersection, col_intersection, row_nearest, col_nearest, qp_energy):
     y, z, core, band = (lax.axis_index(a) for a in ("y", "z", "core", "band"))
-    near = [coarse_kernel] + [shift(coarse_kernel, "band", NB, d) for d in range(1, NB)]
+    near = [coarse_kernel] + [shift(coarse_kernel, "band", NB, d) for d in (2, 1, 3)]
     pick = (band - row_nearest) % NB
     c, v = row_intersection[0, 0], row_intersection[1, 0]
     row_coef = (c[:, None, :, None] * v[None, :, None, :]).reshape(FP, CP).astype(BF16)
@@ -241,6 +249,7 @@
         out_specs=whole(1)[0],
         out_shape=jax.ShapeDtypeStruct((2, CP, 128), BF16),
         compiler_params=limit,
+        cost_estimate=pl.CostEstimate(flops=0, bytes_accessed=0, transcendentals=0),
         name="strip",
     )(pick, *near, row_coef)
 
@@ -255,42 +264,45 @@
     for a, blocks in ((1, 2), (2, 4), (3, 4), (4, 4), (5, 1)):
         places += [(len(places) + b, ((a, 2 * b), (a, 2 * b + 1))) for b in range(blocks)]
 
+    anywhere = pl.BlockSpec(memory_space=pl.ANY)
     got = []
-    for lo, hi in PARTS:
-        used = sorted({a for _, pairs in places[lo:hi] for a, _ in pairs})
-        halves = sorted({pos // HALF for pos in range(lo, hi)})
-        mine = [(pos, tuple((used.index(a), b) for a, b in pairs)) for pos, pairs in places[lo:hi]]
+    for n, (low, high) in enumerate(PARTS):
+        results = []
+        for lo, hi in RANGES[n]:
+            used = sorted({a for _, pairs in places[lo:hi] for a, _ in pairs})
+            halves = sorted({pos // HALF for pos in range(lo, hi)})
+            mine = [(pos, tuple((used.index(a), b) for a, b in pairs)) for pos, pairs in places[lo:hi]]
+            operands = [local, *[f for h in halves for f in factors[2 * h : 2 * h + 2]], *[strips[a] for a in used]]
+            result = pl.pallas_call(
+                functools.partial(result_kernel, mine, halves, lo - low),
+                in_specs=whole(len(operands)) + [anywhere] * len(results),
+                out_specs=anywhere,
+                out_shape=jax.ShapeDtypeStruct((GROUP, high - low, FP, 128), BF16),
+                input_output_aliases={len(operands): 0} if results else {},
+                scratch_shapes=[pltpu.VMEM((hi - lo, GROUP, FP, 128), BF16), pltpu.SemaphoreType.DMA((hi - lo,))],
+                compiler_params=limit,
+                cost_estimate=pl.CostEstimate(flops=COSTS[lo] * 10**9, bytes_accessed=10**6, transcendentals=0),
+                name="result",
+            )(*operands, *results)
+            results = [result]
+            local, result = lax.optimization_barrier((local, result))
+            results = [result]
         if got:
-            local, last = lax.optimization_barrier((local, last))
-        results = pl.pallas_call(
-            functools.partial(result_kernel, mine, halves),
-            in_specs=whole(1 + 2 * len(halves) + len(used)),
-            out_specs=whole(1)[0],
-            out_shape=jax.ShapeDtypeStruct((GROUP, hi - lo, FP, 128), BF16),
-            compiler_params=limit,
-            cost_estimate=pl.CostEstimate(flops=COSTS[len(got)] * 10**9, bytes_accessed=10**6, transcendentals=0),
-            name="result",
-        )(local, *[f for h in halves for f in factors[2 * h : 2 * h + 2]], *[strips[a] for a in used])
-        last = results
-        if got:
-            results, got[-1] = lax.optimization_barrier((results, got[-1]))
-        got.append(lax.all_to_all(results, ("y", "core"), 0, 0, tiled=True).reshape(-1, FP, 128))
+            result, got[-1] = lax.optimization_barrier((result, got[-1]))
+        got.append(lax.all_to_all(result, ("y", "core"), 0, 0, tiled=True).reshape(-1, FP, 128))
 
     first = jnp.where((y == 0) & (z == 0) & (core == 0), band, -1)
-    steps = 4
-    columns = FC * FP
     return pl.pallas_call(
         assemble_kernel,
-        grid=(steps,),
-        in_specs=[
-            smem,
-            smem,
-            *[pl.BlockSpec(memory_space=pl.ANY)] * len(got),
-            pl.BlockSpec((FP, 1), lambda i: (0, 0)),
+        in_specs=[smem, smem, *[anywhere] * len(got), *whole(1)],
+        out_specs=anywhere,
+        out_shape=jax.ShapeDtypeStruct((FP, FC * FP), BF16),
+        scratch_shapes=[
+            pltpu.VMEM((GROUP * NZ, FP, 128), BF16),
+            pltpu.VMEM((FP, FC * FP), BF16),
+            pltpu.SemaphoreType.DMA((len(got),)),
+            pltpu.SemaphoreType.DMA((12,)),
         ],
-        out_specs=pl.BlockSpec((FP, columns // steps), lambda i: (0, i)),
-        out_shape=jax.ShapeDtypeStruct((FP, columns), BF16),
-        scratch_shapes=[pltpu.VMEM((GROUP * NZ, FP, 128), BF16), pltpu.SemaphoreType.DMA((len(got),))],
         compiler_params=limit,
         name="assemble",
     )(block.reshape(FC), first[None], *got, qp_energy[:, None])

time: 105 us -> 104 us (level)
  waiting for transfers between devices: 25.4 us -> 28.8 us
  starting transfers between devices: 61.6 us -> 59.1 us
  Pallas kernels: 13.6 us -> 12.4 us
    all_to_all x3, waiting for transfers between devices: 16.5 us -> 18.5 us  [body(): lax.all_to_all(result, ('y', 'core'), 0, 0, tiled=True).reshape(-1, FP, 128)]
    ppermute x5, starting transfers between devices: 25.3 us -> 23.4 us  [along(): return lax.ppermute(x, ('z', 'core'), pairs)]
    ppermute x5, waiting for transfers between devices: 3.62 us -> 5.01 us  [along(): return lax.ppermute(x, ('z', 'core'), pairs)]
    pallas_call x4 -> x5, Pallas kernels: 9.59 us -> 8.38 us  [the longest x4 5.84 us: body(): pl.pallas_call(functools.partial(result_kernel, mine, halves, lo - low),...]
  transfers between devices with their start and end apart: 13 -> 13, of which waited for: 8 -> 7; matrix products, arithmetic and copies ran while one was open for 2% -> 2% of each run, Pallas kernels for 9% -> 9%
where the time goes in v3:
time: 104 us; the launch traced here: 103 us
  starting transfers between devices  59.1 us (57%)
  waiting for transfers between devices  28.8 us (28%)
  Pallas kernels  12.4 us (12%)
  local copies, waits for them, and re-layouts  1.61 us (2%)
    ppermute x5, starting transfers between devices, along(): return lax.ppermute(x, ('z', 'core'), pairs)  23.4 us
    all_to_all x3, waiting for transfers between devices, body(): lax.all_to_all(result, ('y', 'core'), 0, 0, tiled=True).reshape(-1, FP, 128)  18.5 us
    ppermute x4, starting transfers between devices, shift(): return lax.ppermute(x, axis, [(i, (i + by) % size) for i in range(size)])  17.9 us
    all_to_all x3, starting transfers between devices, body(): lax.all_to_all(result, ('y', 'core'), 0, 0, tiled=True).reshape(-1, FP, 128)  13.2 us
    pallas_call x4, Pallas kernels, body(): pl.pallas_call(functools.partial(result_kernel, mine, halves, lo - low),...  5.84 us
    ppermute x5, waiting for transfers between devices, along(): return lax.ppermute(x, ('z', 'core'), pairs)  5.01 us
    all_to_all x1, starting transfers between devices, body(): request = lax.all_to_all(request, ('y', 'core'), 0, 0, tiled=True)  4.59 us
    all_to_all x1, waiting for transfers between devices, body(): request = lax.all_to_all(request, ('y', 'core'), 0, 0, tiled=True)  4.42 us
  transfers between devices with their start and end apart: 13, of which 7 were waited for; matrix products, arithmetic and copies ran while one was open for 2% of the time, Pallas kernels for 9%

profile of v3, /device:TPU:1, one launch (start us, length us, event | category | flops | bytes accessed | tf_op | source)
XLA Modules:
  0.0 103.0 jit_solution(10298760750101906906)
XLA Ops:
  0.0 5.6 %collective-permute-start = (bf16[144,576]{1,0:T(8,128)(2,1)}, bf16[144,576]{1,0:T(8,128)(2,1)S(1)}, u32[]{:S(2)}, u32[]{:S(2)}) collective-permute-start(bf16[144,576]{1,0:T(8,128)(2,1)} %k0), channel_id=1, source_target_pairs={{0,2},{1,3},{2,0},{3,1},{4,6},{5,7},{6,4},{7,5},{8,10},{9,11},{10,... | collective-permute-start | bytes 497672 | tf_op jit(solution)/shard_map/ppermute | solution.py:198
  5.6 2.2 %collective-permute-start.1 = (bf16[144,576]{1,0:T(8,128)(2,1)}, bf16[144,576]{1,0:T(8,128)(2,1)S(1)}, u32[]{:S(2)}, u32[]{:S(2)}) collective-permute-start(bf16[144,576]{1,0:T(8,128)(2,1)} %k0), channel_id=1, source_target_pairs={{0,1},{1,2},{2,3},{3,0},{4,5},{5,6},{6,7},{7,4},{8,9},{9,10},{10,1... | collective-permute-start | bytes 497672 | tf_op jit(solution)/shard_map/ppermute | solution.py:198
  7.8 4.3 %collective-permute-start.2 = (bf16[144,576]{1,0:T(8,128)(2,1)}, bf16[144,576]{1,0:T(8,128)(2,1)S(1)}, u32[]{:S(2)}, u32[]{:S(2)}) collective-permute-start(bf16[144,576]{1,0:T(8,128)(2,1)} %k0), channel_id=1, source_target_pairs={{0,3},{1,0},{2,1},{3,2},{4,7},{5,4},{6,5},{7,6},{8,11},{9,8},{10,9... | collective-permute-start | bytes 497672 | tf_op jit(solution)/shard_map/ppermute | solution.py:198
  12.8 1.0 fusion
  14.1 0.1 multiply_convert_fusion
  14.2 0.2 convert_element_type.6.coef_ref
  14.5 1.6 %request.1 = (bf16[8,2,16,768]{3,2,1,0:T(8,128)(2,1)}, s32[1,144]{1,0:T(1,128)S(1)}) custom-call(s32[1]{0:T(128)} %bitcast.z_ref, s32[1,144]{1,0:T(1,128)S(1)} %bitcast.20, f32[144,96]{1,0:T(8,128)S(1)} %copy.13.conduction_ref, f32[144,96]{1,0:T(8,128)S(1)} %copy.14.valence_ref), custom_call_target="tpu_custom_call" | custom-call | tf_op jit(solution)/shard_map/request/pallas_call | solution.py:215
  16.1 0.5 strip.1
  16.7 5.8 %collective-permute-start.3 = (bf16[2,144,128]{2,1,0:T(8,128)(2,1)S(1)}, bf16[2,144,128]{2,1,0:T(8,128)(2,1)S(1)}, u32[]{:S(2)}, u32[]{:S(2)}) collective-permute-start(bf16[2,144,128]{2,1,0:T(8,128)(2,1)S(1)} %strip.1), channel_id=1, source_target_pairs={{0,4},{4,0},{1,5},{5,1},{2,6},{6,2},{3,7},{7,3},{8,12},{12,8},{9,1... | collective-permute-start | bytes 221192 | tf_op jit(solution)/shard_map/ppermute | solution.py:198
  22.5 0.9 collective-permute-done.3
  23.4 8.8 %collective-permute-start.4 = (bf16[4,144,128]{2,1,0:T(8,128)(2,1)S(1)}, bf16[4,144,128]{2,1,0:T(8,128)(2,1)S(1)}, u32[]{:S(2)}, u32[]{:S(2)}) collective-permute-start(bf16[4,144,128]{2,1,0:T(8,128)(2,1)S(1)} %pad_maximum_fusion.1.refs_2_), channel_id=1, source_target_pairs={{0,8},{4,124},{8,16},{12,4},{16,24},{20,12},{24,32},{28,20},{32,40... | collective-permute-start | bytes 442376 | tf_op jit(solution)/shard_map/ppermute | solution.py:203
  32.2 4.6 %all-to-all-start = ((bf16[8,2,16,768]{3,2,1,0:T(8,128)(2,1)}), bf16[8,2,16,768]{3,2,1,0:T(8,128)(2,1)S(1)}, u32[]{:S(2)}, u32[]{:S(2)}) async-start(bf16[8,2,16,768]{3,2,1,0:T(8,128)(2,1)} %get-tuple-element.30), calls=%async_computation | async-start | bytes 786432 | tf_op jit(solution)/shard_map/all_to_all | solution.py:232
  36.8 3.6 %collective-permute-start.5 = (bf16[8,144,128]{2,1,0:T(8,128)(2,1)S(1)}, bf16[8,144,128]{2,1,0:T(8,128)(2,1)S(1)}, u32[]{:S(2)}, u32[]{:S(2)}) collective-permute-start(bf16[8,144,128]{2,1,0:T(8,128)(2,1)S(1)} %pad_maximum_fusion), channel_id=1, source_target_pairs={{0,16},{4,116},{8,24},{12,124},{16,32},{20,4},{24,40},{28,12},{32,... | collective-permute-start | bytes 884744 | tf_op jit(solution)/shard_map/ppermute | solution.py:203
  40.4 4.4 %all-to-all-done.x_ref = bf16[8,2,16,768]{3,2,1,0:T(8,128)(2,1)S(1)} async-done(((bf16[8,2,16,768]{3,2,1,0:T(8,128)(2,1)}), bf16[8,2,16,768]{3,2,1,0:T(8,128)(2,1)S(1)}, u32[]{:S(2)}, u32[]{:S(2)}) %all-to-all-start) | async-done | bytes 393248 | tf_op jit(solution)/shard_map/all_to_all | solution.py:232
  44.8 1.9 %expand.1 = (f32[8,96,128]{2,1,0:T(8,128)S(1)}, f32[8,96,128]{2,1,0:T(8,128)S(1)}, f32[8,96,128]{2,1,0:T(8,128)S(1)}, f32[8,96,128]{2,1,0:T(8,128)S(1)}, f32[16,1024]{1,0:T(8,128)S(1)}) custom-call(bf16[8,2,16,768]{3,2,1,0:T(8,128)(2,1)S(1)} %all-to-all-done.x_ref), custom_call_target="tpu_custom_call" | custom-call | tf_op jit(solution)/shard_map/expand/pallas_call | solution.py:234
  46.7 1.3 %result.4.refs_3_ = bf16[8,6,64,128]{3,2,1,0:T(8,128)(2,1)} custom-call(f32[16,1024]{1,0:T(8,128)S(1)} %get-tuple-element.46.local_ref, f32[8,96,128]{2,1,0:T(8,128)S(1)} %get-tuple-element.32.refs_0_, f32[8,96,128]{2,1,0:T(8,128)S(1)} %get-tuple-element.33.refs_1_, bf16[4,144,128]{2,1,0:T(8,128)(2,1)S(1)} %pad_maximum_fusion.1.refs_2_, ...), custom_call_target="tpu_custom_call" | custom-call | bytes 1000000 | tf_op jit(solution)/shard_map/result/pallas_call | solution.py:276
  48.0 3.8 %collective-permute-start.6 = (bf16[8,144,128]{2,1,0:T(8,128)(2,1)S(1)}, bf16[8,144,128]{2,1,0:T(8,128)(2,1)S(1)}, u32[]{:S(2)}, u32[]{:S(2)}) collective-permute-start(bf16[8,144,128]{2,1,0:T(8,128)(2,1)S(1)} %collective-permute-done.5.refs_2_.refs_4_), channel_id=1, source_target_pairs={{0,16},{4,116},{8,24},{12,124},{16,32},{20,4},{24,40},{28,12},{32,... | collective-permute-start | bytes 884744 | tf_op jit(solution)/shard_map/ppermute | solution.py:203
  51.8 1.3 %result.5 = bf16[8,6,64,128]{3,2,1,0:T(8,128)(2,1)} custom-call(f32[16,1024]{1,0:T(8,128)S(1)} %get-tuple-element.46.local_ref, f32[8,96,128]{2,1,0:T(8,128)S(1)} %get-tuple-element.32.refs_0_, f32[8,96,128]{2,1,0:T(8,128)S(1)} %get-tuple-element.33.refs_1_, ...), custom_call_target="tpu_custom_call", output_to_operand_aliasing={{}: (4, {})} | custom-call | flops 10000000000 | bytes 1000000 | tf_op jit(solution)/shard_map/result/pallas_call | solution.py:276
  53.2 4.6 %all-to-all-start.1 = ((bf16[8,6,64,128]{3,2,1,0:T(8,128)(2,1)}), bf16[8,6,64,128]{3,2,1,0:T(8,128)(2,1)S(1)}, u32[]{:S(2)}, u32[]{:S(2)}) async-start(bf16[8,6,64,128]{3,2,1,0:T(8,128)(2,1)} %result.5), calls=%async_computation.1 | async-start | bytes 1572864 | tf_op jit(solution)/shard_map/all_to_all | solution.py:292
  57.7 2.0 %collective-permute-done.6.refs_5_ = bf16[8,144,128]{2,1,0:T(8,128)(2,1)S(1)} collective-permute-done((bf16[8,144,128]{2,1,0:T(8,128)(2,1)S(1)}, bf16[8,144,128]{2,1,0:T(8,128)(2,1)S(1)}, u32[]{:S(2)}, u32[]{:S(2)}) %collective-permute-start.6) | collective-permute-done | bytes 294944 | tf_op jit(solution)/shard_map/ppermute | solution.py:203
  59.8 4.7 %collective-permute-start.7 = (bf16[8,144,128]{2,1,0:T(8,128)(2,1)S(1)}, bf16[8,144,128]{2,1,0:T(8,128)(2,1)S(1)}, u32[]{:S(2)}, u32[]{:S(2)}) collective-permute-start(bf16[8,144,128]{2,1,0:T(8,128)(2,1)S(1)} %collective-permute-done.6.refs_5_), channel_id=1, source_target_pairs={{0,16},{4,116},{8,24},{12,124},{16,32},{20,4},{24,40},{28,12},{32,... | collective-permute-start | bytes 884744 | tf_op jit(solution)/shard_map/ppermute | solution.py:203
  64.5 1.6 %result.6 = bf16[8,5,64,128]{3,2,1,0:T(8,128)(2,1)} custom-call(f32[16,1024]{1,0:T(8,128)S(1)} %get-tuple-element.46.local_ref, f32[8,96,128]{2,1,0:T(8,128)S(1)} %get-tuple-element.32.refs_0_, f32[8,96,128]{2,1,0:T(8,128)S(1)} %get-tuple-element.33.refs_1_, f32[8,96,128]{2,1,0:T(8,128)S(1)} %get-tuple-element.41.refs_2_.refs_0_, ...), custom_call_target="tpu_custom_call" | custom-call | flops 20000000000 | bytes 1000000 | tf_op jit(solution)/shard_map/result/pallas_call | solution.py:276
  66.2 3.9 %all-to-all-done.1 = bf16[8,6,64,128]{3,2,1,0:T(8,128)(2,1)S(1)} async-done(((bf16[8,6,64,128]{3,2,1,0:T(8,128)(2,1)}), bf16[8,6,64,128]{3,2,1,0:T(8,128)(2,1)S(1)}, u32[]{:S(2)}, u32[]{:S(2)}) %all-to-all-start.1) | async-done | bytes 786464 | tf_op jit(solution)/shard_map/all_to_all | solution.py:292
  70.0 4.3 %all-to-all-start.2 = ((bf16[8,5,64,128]{3,2,1,0:T(8,128)(2,1)}), bf16[8,5,64,128]{3,2,1,0:T(8,128)(2,1)S(1)}, u32[]{:S(2)}, u32[]{:S(2)}) async-start(bf16[8,5,64,128]{3,2,1,0:T(8,128)(2,1)} %result.6), calls=%async_computation.2 | async-start | bytes 1310720 | tf_op jit(solution)/shard_map/all_to_all | solution.py:292
  74.3 2.5 %collective-permute-start.8 = (bf16[2,144,128]{2,1,0:T(8,128)(2,1)S(1)}, bf16[2,144,128]{2,1,0:T(8,128)(2,1)S(1)}, u32[]{:S(2)}, u32[]{:S(2)}) collective-permute-start(bf16[2,144,128]{2,1,0:T(8,128)(2,1)S(1)} %slice.20), channel_id=1, source_target_pairs={{0,8},{4,124},{8,16},{12,4},{16,24},{20,12},{24,32},{28,20},{32,40... | collective-permute-start | bytes 221192 | tf_op jit(solution)/shard_map/ppermute | solution.py:203
  76.8 3.0 %collective-permute-done.8.refs_3_ = bf16[2,144,128]{2,1,0:T(8,128)(2,1)S(1)} collective-permute-done((bf16[2,144,128]{2,1,0:T(8,128)(2,1)S(1)}, bf16[2,144,128]{2,1,0:T(8,128)(2,1)S(1)}, u32[]{:S(2)}, u32[]{:S(2)}) %collective-permute-start.8) | collective-permute-done | bytes 73760 | tf_op jit(solution)/shard_map/ppermute | solution.py:203
  79.8 1.6 %result.7 = bf16[8,5,64,128]{3,2,1,0:T(8,128)(2,1)} custom-call(f32[16,1024]{1,0:T(8,128)S(1)} %get-tuple-element.46.local_ref, f32[8,96,128]{2,1,0:T(8,128)S(1)} %get-tuple-element.41.refs_2_.refs_0_, f32[8,96,128]{2,1,0:T(8,128)S(1)} %get-tuple-element.42.refs_3_.refs_1_, bf16[8,144,128]{2,1,0:T(8,128)(2,1)S(1)} %collective-permute-done.7.refs_2_, ...), custom_call_target="tpu_custom_call" | custom-call | flops 4000000000 | bytes 1000000 | tf_op jit(solution)/shard_map/result/pallas_call | solution.py:276
  81.4 3.8 %all-to-all-done.2 = bf16[8,5,64,128]{3,2,1,0:T(8,128)(2,1)S(1)} async-done(((bf16[8,5,64,128]{3,2,1,0:T(8,128)(2,1)}), bf16[8,5,64,128]{3,2,1,0:T(8,128)(2,1)S(1)}, u32[]{:S(2)}, u32[]{:S(2)}) %all-to-all-start.2) | async-done | bytes 655392 | tf_op jit(solution)/shard_map/all_to_all | solution.py:292
  85.2 4.3 %all-to-all-start.3 = ((bf16[8,5,64,128]{3,2,1,0:T(8,128)(2,1)}), bf16[8,5,64,128]{3,2,1,0:T(8,128)(2,1)S(1)}, u32[]{:S(2)}, u32[]{:S(2)}) async-start(bf16[8,5,64,128]{3,2,1,0:T(8,128)(2,1)} %result.7), calls=%async_computation.3 | async-start | bytes 1310720 | tf_op jit(solution)/shard_map/all_to_all | solution.py:292
  89.6 0.1 copy.15.refs_3_
  89.6 10.8 %all-to-all-done.3 = bf16[8,5,64,128]{3,2,1,0:T(8,128)(2,1)S(1)} async-done(((bf16[8,5,64,128]{3,2,1,0:T(8,128)(2,1)}), bf16[8,5,64,128]{3,2,1,0:T(8,128)(2,1)S(1)}, u32[]{:S(2)}, u32[]{:S(2)}) %all-to-all-start.3) | async-done | bytes 655392 | tf_op jit(solution)/shard_map/all_to_all | solution.py:292
  100.5 2.5 %assemble.1 = bf16[64,9216]{1,0:T(8,128)(2,1)} custom-call(s32[144]{0:T(256)S(1)} %bitcast.21, s32[1]{0:T(128)} %bitcast.3.where_ref, bf16[48,64,128]{2,1,0:T(8,128)(2,1)S(1)} %bitcast.17, bf16[40,64,128]{2,1,0:T(8,128)(2,1)S(1)} %bitcast.18, bf16[40,64,128]{2,1,0:T(8,128)(2,1)S(1)} %bitcast.19, f32[64,1]{1,0:T(8,128)S(1)} %copy.15.refs_3_), custom_call_target="tpu_custom_call" | custom-call | tf_op jit(solution)/shard_map/assemble/pallas_call | solution.py:295
  (24 shorter events, 0.4 us)
Async XLA Ops:
  0.0 14.1 %copy-start.2 = (f32[2,1,8,12]{3,2,1,0:T(8,128)S(1)}, f32[2,1,8,12]{3,2,1,0:T(8,128)}, u32[]{:S(2)}) copy-start(f32[2,1,8,12]{3,2,1,0:T(8,128)} %param.7) | copy-start | bytes 2308
  0.0 14.5 %copy-start.1 = (s32[144]{0:T(256)S(1)}, s32[144]{0:T(256)}, u32[]{:S(2)}) copy-start(s32[144]{0:T(256)} %param.10) | copy-start | bytes 1732
  0.0 16.1 %collective-permute-start = (bf16[144,576]{1,0:T(8,128)(2,1)}, bf16[144,576]{1,0:T(8,128)(2,1)S(1)}, u32[]{:S(2)}, u32[]{:S(2)}) collective-permute-start(bf16[144,576]{1,0:T(8,128)(2,1)} %k0), channel_id=1, source_target_pairs={{0,2},{1,3},{2,0},{3,1},{4,6},{5,7},{6,4},{7,5},{8,10},{9,11},{10,... | collective-permute-start | bytes 497672 | tf_op jit(solution)/shard_map/ppermute | solution.py:198
  5.6 10.5 %collective-permute-start.1 = (bf16[144,576]{1,0:T(8,128)(2,1)}, bf16[144,576]{1,0:T(8,128)(2,1)S(1)}, u32[]{:S(2)}, u32[]{:S(2)}) collective-permute-start(bf16[144,576]{1,0:T(8,128)(2,1)} %k0), channel_id=1, source_target_pairs={{0,1},{1,2},{2,3},{3,0},{4,5},{5,6},{6,7},{7,4},{8,9},{9,10},{10,1... | collective-permute-start | bytes 497672 | tf_op jit(solution)/shard_map/ppermute | solution.py:198
  7.8 8.3 %collective-permute-start.2 = (bf16[144,576]{1,0:T(8,128)(2,1)}, bf16[144,576]{1,0:T(8,128)(2,1)S(1)}, u32[]{:S(2)}, u32[]{:S(2)}) collective-permute-start(bf16[144,576]{1,0:T(8,128)(2,1)} %k0), channel_id=1, source_target_pairs={{0,3},{1,0},{2,1},{3,2},{4,7},{5,4},{6,5},{7,6},{8,11},{9,8},{10,9... | collective-permute-start | bytes 497672 | tf_op jit(solution)/shard_map/ppermute | solution.py:198
  12.8 3.4 %copy-start = (bf16[144,576]{1,0:T(8,128)(2,1)S(1)}, bf16[144,576]{1,0:T(8,128)(2,1)}, u32[]{:S(2)}) copy-start(bf16[144,576]{1,0:T(8,128)(2,1)} %k0) | copy-start | bytes 497668
  16.7 6.7 %collective-permute-start.3 = (bf16[2,144,128]{2,1,0:T(8,128)(2,1)S(1)}, bf16[2,144,128]{2,1,0:T(8,128)(2,1)S(1)}, u32[]{:S(2)}, u32[]{:S(2)}) collective-permute-start(bf16[2,144,128]{2,1,0:T(8,128)(2,1)S(1)} %strip.1), channel_id=1, source_target_pairs={{0,4},{4,0},{1,5},{5,1},{2,6},{6,2},{3,7},{7,3},{8,12},{12,8},{9,1... | collective-permute-start | bytes 221192 | tf_op jit(solution)/shard_map/ppermute | solution.py:198
  23.4 13.4 %collective-permute-start.4 = (bf16[4,144,128]{2,1,0:T(8,128)(2,1)S(1)}, bf16[4,144,128]{2,1,0:T(8,128)(2,1)S(1)}, u32[]{:S(2)}, u32[]{:S(2)}) collective-permute-start(bf16[4,144,128]{2,1,0:T(8,128)(2,1)S(1)} %pad_maximum_fusion.1.refs_2_), channel_id=1, source_target_pairs={{0,8},{4,124},{8,16},{12,4},{16,24},{20,12},{24,32},{28,20},{32,40... | collective-permute-start | bytes 442376 | tf_op jit(solution)/shard_map/ppermute | solution.py:203
  32.2 12.7 %all-to-all-start = ((bf16[8,2,16,768]{3,2,1,0:T(8,128)(2,1)}), bf16[8,2,16,768]{3,2,1,0:T(8,128)(2,1)S(1)}, u32[]{:S(2)}, u32[]{:S(2)}) async-start(bf16[8,2,16,768]{3,2,1,0:T(8,128)(2,1)} %get-tuple-element.30), calls=%async_computation | async-start | bytes 786432 | tf_op jit(solution)/shard_map/all_to_all | solution.py:232
  36.8 11.2 %collective-permute-start.5 = (bf16[8,144,128]{2,1,0:T(8,128)(2,1)S(1)}, bf16[8,144,128]{2,1,0:T(8,128)(2,1)S(1)}, u32[]{:S(2)}, u32[]{:S(2)}) collective-permute-start(bf16[8,144,128]{2,1,0:T(8,128)(2,1)S(1)} %pad_maximum_fusion), channel_id=1, source_target_pairs={{0,16},{4,116},{8,24},{12,124},{16,32},{20,4},{24,40},{28,12},{32,... | collective-permute-start | bytes 884744 | tf_op jit(solution)/shard_map/ppermute | solution.py:203
  48.0 11.7 %collective-permute-start.6 = (bf16[8,144,128]{2,1,0:T(8,128)(2,1)S(1)}, bf16[8,144,128]{2,1,0:T(8,128)(2,1)S(1)}, u32[]{:S(2)}, u32[]{:S(2)}) collective-permute-start(bf16[8,144,128]{2,1,0:T(8,128)(2,1)S(1)} %collective-permute-done.5.refs_2_.refs_4_), channel_id=1, source_target_pairs={{0,16},{4,116},{8,24},{12,124},{16,32},{20,4},{24,40},{28,12},{32,... | collective-permute-start | bytes 884744 | tf_op jit(solution)/shard_map/ppermute | solution.py:203
  53.2 16.9 %all-to-all-start.1 = ((bf16[8,6,64,128]{3,2,1,0:T(8,128)(2,1)}), bf16[8,6,64,128]{3,2,1,0:T(8,128)(2,1)S(1)}, u32[]{:S(2)}, u32[]{:S(2)}) async-start(bf16[8,6,64,128]{3,2,1,0:T(8,128)(2,1)} %result.5), calls=%async_computation.1 | async-start | bytes 1572864 | tf_op jit(solution)/shard_map/all_to_all | solution.py:292
  59.8 14.6 %collective-permute-start.7 = (bf16[8,144,128]{2,1,0:T(8,128)(2,1)S(1)}, bf16[8,144,128]{2,1,0:T(8,128)(2,1)S(1)}, u32[]{:S(2)}, u32[]{:S(2)}) collective-permute-start(bf16[8,144,128]{2,1,0:T(8,128)(2,1)S(1)} %collective-permute-done.6.refs_5_), channel_id=1, source_target_pairs={{0,16},{4,116},{8,24},{12,124},{16,32},{20,4},{24,40},{28,12},{32,... | collective-permute-start | bytes 884744 | tf_op jit(solution)/shard_map/ppermute | solution.py:203
  70.0 15.2 %all-to-all-start.2 = ((bf16[8,5,64,128]{3,2,1,0:T(8,128)(2,1)}), bf16[8,5,64,128]{3,2,1,0:T(8,128)(2,1)S(1)}, u32[]{:S(2)}, u32[]{:S(2)}) async-start(bf16[8,5,64,128]{3,2,1,0:T(8,128)(2,1)} %result.6), calls=%async_computation.2 | async-start | bytes 1310720 | tf_op jit(solution)/shard_map/all_to_all | solution.py:292
  74.3 5.5 %collective-permute-start.8 = (bf16[2,144,128]{2,1,0:T(8,128)(2,1)S(1)}, bf16[2,144,128]{2,1,0:T(8,128)(2,1)S(1)}, u32[]{:S(2)}, u32[]{:S(2)}) collective-permute-start(bf16[2,144,128]{2,1,0:T(8,128)(2,1)S(1)} %slice.20), channel_id=1, source_target_pairs={{0,8},{4,124},{8,16},{12,4},{16,24},{20,12},{24,32},{28,20},{32,40... | collective-permute-start | bytes 221192 | tf_op jit(solution)/shard_map/ppermute | solution.py:203
  81.4 8.1 %copy-start.3 = (f32[64]{0:T(128)S(1)}, f32[64]{0:T(128)}, u32[]{:S(2)}) copy-start(f32[64]{0:T(128)} %param.11) | copy-start | bytes 772
  85.2 15.2 %all-to-all-start.3 = ((bf16[8,5,64,128]{3,2,1,0:T(8,128)(2,1)}), bf16[8,5,64,128]{3,2,1,0:T(8,128)(2,1)S(1)}, u32[]{:S(2)}, u32[]{:S(2)}) async-start(bf16[8,5,64,128]{3,2,1,0:T(8,128)(2,1)} %result.7), calls=%async_computation.3 | async-start | bytes 1310720 | tf_op jit(solution)/shard_map/all_to_all | solution.py:292

commit v4 on v3

--- a/solution.py
+++ b/solution.py
@@ -19,9 +19,9 @@
 HELD = 4
 CAP = 2
 PARTS = ((0, 6), (6, 11), (11, 16))
-RANGES = (((0, 3), (3, 6)), ((6, 11),), ((11, 16),))
+RANGES = (((0, 3), (3, 6)), ((6, 11),), ((11, 15), (15, 16)))
 HALF = NZ // 2
-COSTS = {0: 0, 3: 10, 6: 20, 11: 4}
+COSTS = {0: 0, 3: 10, 6: 20, 11: 4, 15: 0}
 F32 = jnp.float32
 BF16 = jnp.bfloat16
 

time: 104 us -> 104 us (level)
  waiting for transfers between devices: 28.8 us -> 27 us
  Pallas kernels: 12.4 us -> 14.2 us
    pallas_call x4 -> x5, Pallas kernels: 5.84 us -> 7.64 us  [body(): pl.pallas_call(functools.partial(result_kernel, mine, halves, lo - low),...]
    ppermute x5, waiting for transfers between devices: 5.01 us -> 3.67 us  [along(): return lax.ppermute(x, ('z', 'core'), pairs)]
  transfers between devices with their start and end apart: 13 -> 13, of which waited for: 7 -> 7; matrix products, arithmetic and copies ran while one was open for 2% -> 2% of each run, Pallas kernels for 9% -> 11%
where the time goes in v4:
time: 104 us; the launch traced here: 103 us
  starting transfers between devices  59.1 us (57%)
  waiting for transfers between devices  27 us (26%)
  Pallas kernels  14.2 us (14%)
  local copies, waits for them, and re-layouts  1.61 us (2%)
    ppermute x5, starting transfers between devices, along(): return lax.ppermute(x, ('z', 'core'), pairs)  23.4 us
    all_to_all x3, waiting for transfers between devices, body(): lax.all_to_all(result, ('y', 'core'), 0, 0, tiled=True).reshape(-1, FP, 128)  18 us
    ppermute x4, starting transfers between devices, shift(): return lax.ppermute(x, axis, [(i, (i + by) % size) for i in range(size)])  17.9 us
    all_to_all x3, starting transfers between devices, body(): lax.all_to_all(result, ('y', 'core'), 0, 0, tiled=True).reshape(-1, FP, 128)  13.2 us
    pallas_call x5, Pallas kernels, body(): pl.pallas_call(functools.partial(result_kernel, mine, halves, lo - low),...  7.64 us
    all_to_all x1, starting transfers between devices, body(): request = lax.all_to_all(request, ('y', 'core'), 0, 0, tiled=True)  4.59 us
    all_to_all x1, waiting for transfers between devices, body(): request = lax.all_to_all(request, ('y', 'core'), 0, 0, tiled=True)  4.42 us
    ppermute x5, waiting for transfers between devices, along(): return lax.ppermute(x, ('z', 'core'), pairs)  3.67 us
  transfers between devices with their start and end apart: 13, of which 7 were waited for; matrix products, arithmetic and copies ran while one was open for 2% of the time, Pallas kernels for 11%

profile of v4, /device:TPU:1, one launch (start us, length us, event | category | flops | bytes accessed | tf_op | source)
XLA Modules:
  0.0 103.0 jit_solution(12480775825661705502)
XLA Ops:
  0.0 5.6 %collective-permute-start = (bf16[144,576]{1,0:T(8,128)(2,1)}, bf16[144,576]{1,0:T(8,128)(2,1)S(1)}, u32[]{:S(2)}, u32[]{:S(2)}) collective-permute-start(bf16[144,576]{1,0:T(8,128)(2,1)} %k0), channel_id=1, source_target_pairs={{0,2},{1,3},{2,0},{3,1},{4,6},{5,7},{6,4},{7,5},{8,10},{9,11},{10,... | collective-permute-start | bytes 497672 | tf_op jit(solution)/shard_map/ppermute | solution.py:198
  5.6 2.2 %collective-permute-start.1 = (bf16[144,576]{1,0:T(8,128)(2,1)}, bf16[144,576]{1,0:T(8,128)(2,1)S(1)}, u32[]{:S(2)}, u32[]{:S(2)}) collective-permute-start(bf16[144,576]{1,0:T(8,128)(2,1)} %k0), channel_id=1, source_target_pairs={{0,1},{1,2},{2,3},{3,0},{4,5},{5,6},{6,7},{7,4},{8,9},{9,10},{10,1... | collective-permute-start | bytes 497672 | tf_op jit(solution)/shard_map/ppermute | solution.py:198
  7.8 4.3 %collective-permute-start.2 = (bf16[144,576]{1,0:T(8,128)(2,1)}, bf16[144,576]{1,0:T(8,128)(2,1)S(1)}, u32[]{:S(2)}, u32[]{:S(2)}) collective-permute-start(bf16[144,576]{1,0:T(8,128)(2,1)} %k0), channel_id=1, source_target_pairs={{0,3},{1,0},{2,1},{3,2},{4,7},{5,4},{6,5},{7,6},{8,11},{9,8},{10,9... | collective-permute-start | bytes 497672 | tf_op jit(solution)/shard_map/ppermute | solution.py:198
  12.8 1.0 fusion
  14.1 0.1 multiply_convert_fusion
  14.2 0.2 convert_element_type.6.coef_ref
  14.5 1.6 %request.1 = (bf16[8,2,16,768]{3,2,1,0:T(8,128)(2,1)}, s32[1,144]{1,0:T(1,128)S(1)}) custom-call(s32[1]{0:T(128)} %bitcast.z_ref, s32[1,144]{1,0:T(1,128)S(1)} %bitcast.20, f32[144,96]{1,0:T(8,128)S(1)} %copy.14.conduction_ref, f32[144,96]{1,0:T(8,128)S(1)} %copy.15.valence_ref), custom_call_target="tpu_custom_call" | custom-call | tf_op jit(solution)/shard_map/request/pallas_call | solution.py:215
  16.1 0.5 strip.1
  16.7 5.8 %collective-permute-start.3 = (bf16[2,144,128]{2,1,0:T(8,128)(2,1)S(1)}, bf16[2,144,128]{2,1,0:T(8,128)(2,1)S(1)}, u32[]{:S(2)}, u32[]{:S(2)}) collective-permute-start(bf16[2,144,128]{2,1,0:T(8,128)(2,1)S(1)} %strip.1), channel_id=1, source_target_pairs={{0,4},{4,0},{1,5},{5,1},{2,6},{6,2},{3,7},{7,3},{8,12},{12,8},{9,1... | collective-permute-start | bytes 221192 | tf_op jit(solution)/shard_map/ppermute | solution.py:198
  22.5 0.9 collective-permute-done.3
  23.4 8.8 %collective-permute-start.4 = (bf16[4,144,128]{2,1,0:T(8,128)(2,1)S(1)}, bf16[4,144,128]{2,1,0:T(8,128)(2,1)S(1)}, u32[]{:S(2)}, u32[]{:S(2)}) collective-permute-start(bf16[4,144,128]{2,1,0:T(8,128)(2,1)S(1)} %pad_maximum_fusion.1.refs_2_), channel_id=1, source_target_pairs={{0,8},{4,124},{8,16},{12,4},{16,24},{20,12},{24,32},{28,20},{32,40... | collective-permute-start | bytes 442376 | tf_op jit(solution)/shard_map/ppermute | solution.py:203
  32.2 4.6 %all-to-all-start = ((bf16[8,2,16,768]{3,2,1,0:T(8,128)(2,1)}), bf16[8,2,16,768]{3,2,1,0:T(8,128)(2,1)S(1)}, u32[]{:S(2)}, u32[]{:S(2)}) async-start(bf16[8,2,16,768]{3,2,1,0:T(8,128)(2,1)} %get-tuple-element.32), calls=%async_computation | async-start | bytes 786432 | tf_op jit(solution)/shard_map/all_to_all | solution.py:232
  36.8 3.6 %collective-permute-start.5 = (bf16[8,144,128]{2,1,0:T(8,128)(2,1)S(1)}, bf16[8,144,128]{2,1,0:T(8,128)(2,1)S(1)}, u32[]{:S(2)}, u32[]{:S(2)}) collective-permute-start(bf16[8,144,128]{2,1,0:T(8,128)(2,1)S(1)} %pad_maximum_fusion), channel_id=1, source_target_pairs={{0,16},{4,116},{8,24},{12,124},{16,32},{20,4},{24,40},{28,12},{32,... | collective-permute-start | bytes 884744 | tf_op jit(solution)/shard_map/ppermute | solution.py:203
  40.4 4.4 %all-to-all-done.x_ref = bf16[8,2,16,768]{3,2,1,0:T(8,128)(2,1)S(1)} async-done(((bf16[8,2,16,768]{3,2,1,0:T(8,128)(2,1)}), bf16[8,2,16,768]{3,2,1,0:T(8,128)(2,1)S(1)}, u32[]{:S(2)}, u32[]{:S(2)}) %all-to-all-start) | async-done | bytes 393248 | tf_op jit(solution)/shard_map/all_to_all | solution.py:232
  44.8 1.9 %expand.1 = (f32[8,96,128]{2,1,0:T(8,128)S(1)}, f32[8,96,128]{2,1,0:T(8,128)S(1)}, f32[8,96,128]{2,1,0:T(8,128)S(1)}, f32[8,96,128]{2,1,0:T(8,128)S(1)}, f32[16,1024]{1,0:T(8,128)S(1)}) custom-call(bf16[8,2,16,768]{3,2,1,0:T(8,128)(2,1)S(1)} %all-to-all-done.x_ref), custom_call_target="tpu_custom_call" | custom-call | tf_op jit(solution)/shard_map/expand/pallas_call | solution.py:234
  46.7 1.3 %result.5.refs_3_ = bf16[8,6,64,128]{3,2,1,0:T(8,128)(2,1)} custom-call(f32[16,1024]{1,0:T(8,128)S(1)} %get-tuple-element.49.local_ref, f32[8,96,128]{2,1,0:T(8,128)S(1)} %get-tuple-element.34.refs_0_, f32[8,96,128]{2,1,0:T(8,128)S(1)} %get-tuple-element.35.refs_1_, bf16[4,144,128]{2,1,0:T(8,128)(2,1)S(1)} %pad_maximum_fusion.1.refs_2_, ...), custom_call_target="tpu_custom_call" | custom-call | bytes 1000000 | tf_op jit(solution)/shard_map/result/pallas_call | solution.py:276
  48.0 3.8 %collective-permute-start.6 = (bf16[8,144,128]{2,1,0:T(8,128)(2,1)S(1)}, bf16[8,144,128]{2,1,0:T(8,128)(2,1)}, u32[]{:S(2)}, u32[]{:S(2)}) collective-permute-start(bf16[8,144,128]{2,1,0:T(8,128)(2,1)S(1)} %collective-permute-done.5.refs_2_.refs_4_), channel_id=1, source_target_pairs={{0,16},{4,116},{8,24},{12,124},{16,32},{20,4},{24,40},{28,12},{32,... | collective-permute-start | bytes 884744 | tf_op jit(solution)/shard_map/ppermute | solution.py:203
  51.8 1.3 %result.6 = bf16[8,6,64,128]{3,2,1,0:T(8,128)(2,1)} custom-call(f32[16,1024]{1,0:T(8,128)S(1)} %get-tuple-element.49.local_ref, f32[8,96,128]{2,1,0:T(8,128)S(1)} %get-tuple-element.34.refs_0_, f32[8,96,128]{2,1,0:T(8,128)S(1)} %get-tuple-element.35.refs_1_, ...), custom_call_target="tpu_custom_call", output_to_operand_aliasing={{}: (4, {})} | custom-call | flops 10000000000 | bytes 1000000 | tf_op jit(solution)/shard_map/result/pallas_call | solution.py:276
  53.2 4.6 %all-to-all-start.1 = ((bf16[8,6,64,128]{3,2,1,0:T(8,128)(2,1)}), bf16[8,6,64,128]{3,2,1,0:T(8,128)(2,1)S(1)}, u32[]{:S(2)}, u32[]{:S(2)}) async-start(bf16[8,6,64,128]{3,2,1,0:T(8,128)(2,1)} %result.6), calls=%async_computation.1 | async-start | bytes 1572864 | tf_op jit(solution)/shard_map/all_to_all | solution.py:292
  57.7 2.1 %collective-permute-done.6.refs_5_ = bf16[8,144,128]{2,1,0:T(8,128)(2,1)} collective-permute-done((bf16[8,144,128]{2,1,0:T(8,128)(2,1)S(1)}, bf16[8,144,128]{2,1,0:T(8,128)(2,1)}, u32[]{:S(2)}, u32[]{:S(2)}) %collective-permute-start.6) | collective-permute-done | bytes 294944 | tf_op jit(solution)/shard_map/ppermute | solution.py:203
  59.9 4.7 %collective-permute-start.7 = (bf16[8,144,128]{2,1,0:T(8,128)(2,1)}, bf16[8,144,128]{2,1,0:T(8,128)(2,1)S(1)}, u32[]{:S(2)}, u32[]{:S(2)}) collective-permute-start(bf16[8,144,128]{2,1,0:T(8,128)(2,1)} %collective-permute-done.6.refs_5_), channel_id=1, source_target_pairs={{0,16},{4,116},{8,24},{12,124},{16,32},{20,4},{24,40},{28,12},{32,... | collective-permute-start | bytes 884744 | tf_op jit(solution)/shard_map/ppermute | solution.py:203
  64.6 2.6 %result.7 = bf16[8,5,64,128]{3,2,1,0:T(8,128)(2,1)} custom-call(f32[16,1024]{1,0:T(8,128)S(1)} %get-tuple-element.49.local_ref, f32[8,96,128]{2,1,0:T(8,128)S(1)} %get-tuple-element.34.refs_0_, f32[8,96,128]{2,1,0:T(8,128)S(1)} %get-tuple-element.35.refs_1_, f32[8,96,128]{2,1,0:T(8,128)S(1)} %get-tuple-element.43.refs_2_.refs_0_, ...), custom_call_target="tpu_custom_call" | custom-call | flops 20000000000 | bytes 1000000 | tf_op jit(solution)/shard_map/result/pallas_call | solution.py:276
  67.2 2.8 %all-to-all-done.1 = bf16[8,6,64,128]{3,2,1,0:T(8,128)(2,1)S(1)} async-done(((bf16[8,6,64,128]{3,2,1,0:T(8,128)(2,1)}), bf16[8,6,64,128]{3,2,1,0:T(8,128)(2,1)S(1)}, u32[]{:S(2)}, u32[]{:S(2)}) %all-to-all-start.1) | async-done | bytes 786464 | tf_op jit(solution)/shard_map/all_to_all | solution.py:292
  70.0 4.3 %all-to-all-start.2 = ((bf16[8,5,64,128]{3,2,1,0:T(8,128)(2,1)}), bf16[8,5,64,128]{3,2,1,0:T(8,128)(2,1)S(1)}, u32[]{:S(2)}, u32[]{:S(2)}) async-start(bf16[8,5,64,128]{3,2,1,0:T(8,128)(2,1)} %result.7), calls=%async_computation.2 | async-start | bytes 1310720 | tf_op jit(solution)/shard_map/all_to_all | solution.py:292
  74.3 2.5 %collective-permute-start.8 = (bf16[2,144,128]{2,1,0:T(8,128)(2,1)S(1)}, bf16[2,144,128]{2,1,0:T(8,128)(2,1)S(1)}, u32[]{:S(2)}, u32[]{:S(2)}) collective-permute-start(bf16[2,144,128]{2,1,0:T(8,128)(2,1)S(1)} %slice.20), channel_id=1, source_target_pairs={{0,8},{4,124},{8,16},{12,4},{16,24},{20,12},{24,32},{28,20},{32,40... | collective-permute-start | bytes 221192 | tf_op jit(solution)/shard_map/ppermute | solution.py:203
  76.8 1.4 %result.8.refs_3_ = bf16[8,5,64,128]{3,2,1,0:T(8,128)(2,1)} custom-call(f32[16,1024]{1,0:T(8,128)S(1)} %get-tuple-element.49.local_ref, f32[8,96,128]{2,1,0:T(8,128)S(1)} %get-tuple-element.43.refs_2_.refs_0_, f32[8,96,128]{2,1,0:T(8,128)S(1)} %get-tuple-element.44.refs_3_.refs_1_, bf16[8,144,128]{2,1,0:T(8,128)(2,1)S(1)} %collective-permute-done.7.refs_2_), custom_call_target="tpu_custom_call" | custom-call | flops 4000000000 | bytes 1000000 | tf_op jit(solution)/shard_map/result/pallas_call | solution.py:276
  78.3 1.5 %collective-permute-done.8.refs_2_ = bf16[2,144,128]{2,1,0:T(8,128)(2,1)S(1)} collective-permute-done((bf16[2,144,128]{2,1,0:T(8,128)(2,1)S(1)}, bf16[2,144,128]{2,1,0:T(8,128)(2,1)S(1)}, u32[]{:S(2)}, u32[]{:S(2)}) %collective-permute-start.8) | collective-permute-done | bytes 73760 | tf_op jit(solution)/shard_map/ppermute | solution.py:203
  79.8 1.0 result.9
  80.8 4.4 %all-to-all-done.2 = bf16[8,5,64,128]{3,2,1,0:T(8,128)(2,1)S(1)} async-done(((bf16[8,5,64,128]{3,2,1,0:T(8,128)(2,1)}), bf16[8,5,64,128]{3,2,1,0:T(8,128)(2,1)S(1)}, u32[]{:S(2)}, u32[]{:S(2)}) %all-to-all-start.2) | async-done | bytes 655392 | tf_op jit(solution)/shard_map/all_to_all | solution.py:292
  85.2 4.3 %all-to-all-start.3 = ((bf16[8,5,64,128]{3,2,1,0:T(8,128)(2,1)}), bf16[8,5,64,128]{3,2,1,0:T(8,128)(2,1)S(1)}, u32[]{:S(2)}, u32[]{:S(2)}) async-start(bf16[8,5,64,128]{3,2,1,0:T(8,128)(2,1)} %result.9), calls=%async_computation.3 | async-start | bytes 1310720 | tf_op jit(solution)/shard_map/all_to_all | solution.py:292
  89.6 10.8 %all-to-all-done.3 = bf16[8,5,64,128]{3,2,1,0:T(8,128)(2,1)S(1)} async-done(((bf16[8,5,64,128]{3,2,1,0:T(8,128)(2,1)}), bf16[8,5,64,128]{3,2,1,0:T(8,128)(2,1)S(1)}, u32[]{:S(2)}, u32[]{:S(2)}) %all-to-all-start.3) | async-done | bytes 655392 | tf_op jit(solution)/shard_map/all_to_all | solution.py:292
  100.5 2.5 %assemble.1 = bf16[64,9216]{1,0:T(8,128)(2,1)} custom-call(s32[144]{0:T(256)S(1)} %bitcast.21, s32[1]{0:T(128)} %bitcast.3.where_ref, bf16[48,64,128]{2,1,0:T(8,128)(2,1)S(1)} %bitcast.17, bf16[40,64,128]{2,1,0:T(8,128)(2,1)S(1)} %bitcast.18, bf16[40,64,128]{2,1,0:T(8,128)(2,1)S(1)} %bitcast.19, f32[64,1]{1,0:T(8,128)S(1)} %copy.16.refs_3_), custom_call_target="tpu_custom_call" | custom-call | tf_op jit(solution)/shard_map/assemble/pallas_call | solution.py:295
  (25 shorter events, 0.5 us)
Async XLA Ops:
  0.0 14.1 %copy-start.2 = (f32[2,1,8,12]{3,2,1,0:T(8,128)S(1)}, f32[2,1,8,12]{3,2,1,0:T(8,128)}, u32[]{:S(2)}) copy-start(f32[2,1,8,12]{3,2,1,0:T(8,128)} %param.7) | copy-start | bytes 2308
  0.0 14.5 %copy-start.1 = (s32[144]{0:T(256)S(1)}, s32[144]{0:T(256)}, u32[]{:S(2)}) copy-start(s32[144]{0:T(256)} %param.10) | copy-start | bytes 1732
  0.0 16.1 %collective-permute-start = (bf16[144,576]{1,0:T(8,128)(2,1)}, bf16[144,576]{1,0:T(8,128)(2,1)S(1)}, u32[]{:S(2)}, u32[]{:S(2)}) collective-permute-start(bf16[144,576]{1,0:T(8,128)(2,1)} %k0), channel_id=1, source_target_pairs={{0,2},{1,3},{2,0},{3,1},{4,6},{5,7},{6,4},{7,5},{8,10},{9,11},{10,... | collective-permute-start | bytes 497672 | tf_op jit(solution)/shard_map/ppermute | solution.py:198
  5.6 10.5 %collective-permute-start.1 = (bf16[144,576]{1,0:T(8,128)(2,1)}, bf16[144,576]{1,0:T(8,128)(2,1)S(1)}, u32[]{:S(2)}, u32[]{:S(2)}) collective-permute-start(bf16[144,576]{1,0:T(8,128)(2,1)} %k0), channel_id=1, source_target_pairs={{0,1},{1,2},{2,3},{3,0},{4,5},{5,6},{6,7},{7,4},{8,9},{9,10},{10,1... | collective-permute-start | bytes 497672 | tf_op jit(solution)/shard_map/ppermute | solution.py:198
  7.8 8.3 %collective-permute-start.2 = (bf16[144,576]{1,0:T(8,128)(2,1)}, bf16[144,576]{1,0:T(8,128)(2,1)S(1)}, u32[]{:S(2)}, u32[]{:S(2)}) collective-permute-start(bf16[144,576]{1,0:T(8,128)(2,1)} %k0), channel_id=1, source_target_pairs={{0,3},{1,0},{2,1},{3,2},{4,7},{5,4},{6,5},{7,6},{8,11},{9,8},{10,9... | collective-permute-start | bytes 497672 | tf_op jit(solution)/shard_map/ppermute | solution.py:198
  12.8 3.4 %copy-start = (bf16[144,576]{1,0:T(8,128)(2,1)S(1)}, bf16[144,576]{1,0:T(8,128)(2,1)}, u32[]{:S(2)}) copy-start(bf16[144,576]{1,0:T(8,128)(2,1)} %k0) | copy-start | bytes 497668
  16.7 6.7 %collective-permute-start.3 = (bf16[2,144,128]{2,1,0:T(8,128)(2,1)S(1)}, bf16[2,144,128]{2,1,0:T(8,128)(2,1)S(1)}, u32[]{:S(2)}, u32[]{:S(2)}) collective-permute-start(bf16[2,144,128]{2,1,0:T(8,128)(2,1)S(1)} %strip.1), channel_id=1, source_target_pairs={{0,4},{4,0},{1,5},{5,1},{2,6},{6,2},{3,7},{7,3},{8,12},{12,8},{9,1... | collective-permute-start | bytes 221192 | tf_op jit(solution)/shard_map/ppermute | solution.py:198
  23.4 13.4 %collective-permute-start.4 = (bf16[4,144,128]{2,1,0:T(8,128)(2,1)S(1)}, bf16[4,144,128]{2,1,0:T(8,128)(2,1)S(1)}, u32[]{:S(2)}, u32[]{:S(2)}) collective-permute-start(bf16[4,144,128]{2,1,0:T(8,128)(2,1)S(1)} %pad_maximum_fusion.1.refs_2_), channel_id=1, source_target_pairs={{0,8},{4,124},{8,16},{12,4},{16,24},{20,12},{24,32},{28,20},{32,40... | collective-permute-start | bytes 442376 | tf_op jit(solution)/shard_map/ppermute | solution.py:203
  32.2 12.7 %all-to-all-start = ((bf16[8,2,16,768]{3,2,1,0:T(8,128)(2,1)}), bf16[8,2,16,768]{3,2,1,0:T(8,128)(2,1)S(1)}, u32[]{:S(2)}, u32[]{:S(2)}) async-start(bf16[8,2,16,768]{3,2,1,0:T(8,128)(2,1)} %get-tuple-element.32), calls=%async_computation | async-start | bytes 786432 | tf_op jit(solution)/shard_map/all_to_all | solution.py:232
  36.8 11.2 %collective-permute-start.5 = (bf16[8,144,128]{2,1,0:T(8,128)(2,1)S(1)}, bf16[8,144,128]{2,1,0:T(8,128)(2,1)S(1)}, u32[]{:S(2)}, u32[]{:S(2)}) collective-permute-start(bf16[8,144,128]{2,1,0:T(8,128)(2,1)S(1)} %pad_maximum_fusion), channel_id=1, source_target_pairs={{0,16},{4,116},{8,24},{12,124},{16,32},{20,4},{24,40},{28,12},{32,... | collective-permute-start | bytes 884744 | tf_op jit(solution)/shard_map/ppermute | solution.py:203
  48.0 11.8 %collective-permute-start.6 = (bf16[8,144,128]{2,1,0:T(8,128)(2,1)S(1)}, bf16[8,144,128]{2,1,0:T(8,128)(2,1)}, u32[]{:S(2)}, u32[]{:S(2)}) collective-permute-start(bf16[8,144,128]{2,1,0:T(8,128)(2,1)S(1)} %collective-permute-done.5.refs_2_.refs_4_), channel_id=1, source_target_pairs={{0,16},{4,116},{8,24},{12,124},{16,32},{20,4},{24,40},{28,12},{32,... | collective-permute-start | bytes 884744 | tf_op jit(solution)/shard_map/ppermute | solution.py:203
  53.2 16.9 %all-to-all-start.1 = ((bf16[8,6,64,128]{3,2,1,0:T(8,128)(2,1)}), bf16[8,6,64,128]{3,2,1,0:T(8,128)(2,1)S(1)}, u32[]{:S(2)}, u32[]{:S(2)}) async-start(bf16[8,6,64,128]{3,2,1,0:T(8,128)(2,1)} %result.6), calls=%async_computation.1 | async-start | bytes 1572864 | tf_op jit(solution)/shard_map/all_to_all | solution.py:292
  59.9 14.5 %collective-permute-start.7 = (bf16[8,144,128]{2,1,0:T(8,128)(2,1)}, bf16[8,144,128]{2,1,0:T(8,128)(2,1)S(1)}, u32[]{:S(2)}, u32[]{:S(2)}) collective-permute-start(bf16[8,144,128]{2,1,0:T(8,128)(2,1)} %collective-permute-done.6.refs_5_), channel_id=1, source_target_pairs={{0,16},{4,116},{8,24},{12,124},{16,32},{20,4},{24,40},{28,12},{32,... | collective-permute-start | bytes 884744 | tf_op jit(solution)/shard_map/ppermute | solution.py:203
  70.0 15.2 %all-to-all-start.2 = ((bf16[8,5,64,128]{3,2,1,0:T(8,128)(2,1)}), bf16[8,5,64,128]{3,2,1,0:T(8,128)(2,1)S(1)}, u32[]{:S(2)}, u32[]{:S(2)}) async-start(bf16[8,5,64,128]{3,2,1,0:T(8,128)(2,1)} %result.7), calls=%async_computation.2 | async-start | bytes 1310720 | tf_op jit(solution)/shard_map/all_to_all | solution.py:292
  74.3 5.5 %collective-permute-start.8 = (bf16[2,144,128]{2,1,0:T(8,128)(2,1)S(1)}, bf16[2,144,128]{2,1,0:T(8,128)(2,1)S(1)}, u32[]{:S(2)}, u32[]{:S(2)}) collective-permute-start(bf16[2,144,128]{2,1,0:T(8,128)(2,1)S(1)} %slice.20), channel_id=1, source_target_pairs={{0,8},{4,124},{8,16},{12,4},{16,24},{20,12},{24,32},{28,20},{32,40... | collective-permute-start | bytes 221192 | tf_op jit(solution)/shard_map/ppermute | solution.py:203
  80.8 8.7 %copy-start.3 = (f32[64]{0:T(128)S(1)}, f32[64]{0:T(128)}, u32[]{:S(2)}) copy-start(f32[64]{0:T(128)} %param.11) | copy-start | bytes 772
  85.2 15.2 %all-to-all-start.3 = ((bf16[8,5,64,128]{3,2,1,0:T(8,128)(2,1)}), bf16[8,5,64,128]{3,2,1,0:T(8,128)(2,1)S(1)}, u32[]{:S(2)}, u32[]{:S(2)}) async-start(bf16[8,5,64,128]{3,2,1,0:T(8,128)(2,1)} %result.9), calls=%async_computation.3 | async-start | bytes 1310720 | tf_op jit(solution)/shard_map/all_to_all | solution.py:292

commit v5 on v4

--- a/solution.py
+++ b/solution.py
@@ -18,10 +18,10 @@
 FC = 144
 HELD = 4
 CAP = 2
-PARTS = ((0, 6), (6, 11), (11, 16))
-RANGES = (((0, 3), (3, 6)), ((6, 11),), ((11, 15), (15, 16)))
+PARTS = ((0, 5), (5, 11), (11, 16))
+RANGES = (((0, 3), (3, 5)), ((5, 7), (7, 11)), ((11, 15), (15, 16)))
 HALF = NZ // 2
-COSTS = {0: 0, 3: 10, 6: 20, 11: 4, 15: 0}
+COSTS = {0: 0, 3: 10, 5: 0, 7: 20, 11: 4, 15: 0}
 F32 = jnp.float32
 BF16 = jnp.bfloat16
 

time: 104 us -> 115 us (1.11)
  starting transfers between devices: 59.1 us -> 65.5 us
  waiting for transfers between devices: 27 us -> 32.3 us
    all_to_all x3, starting transfers between devices: 13.2 us -> 18.1 us  [body(): lax.all_to_all(result, ('y', 'core'), 0, 0, tiled=True).reshape(-1, FP, 128)]
    ppermute x5, waiting for transfers between devices: 3.67 us -> 7.74 us  [along(): return lax.ppermute(x, ('z', 'core'), pairs)]
    ppermute x5, starting transfers between devices: 23.4 us -> 25 us  [along(): return lax.ppermute(x, ('z', 'core'), pairs)]
    all_to_all x3, waiting for transfers between devices: 18 us -> 19.2 us  [body(): lax.all_to_all(result, ('y', 'core'), 0, 0, tiled=True).reshape(-1, FP, 128)]
    pallas_call x5 -> x6, Pallas kernels: 7.64 us -> 7.55 us  [body(): pl.pallas_call(functools.partial(result_kernel, mine, halves, lo - low),...]
  transfers between devices with their start and end apart: 13 -> 13, of which waited for: 7 -> 7; matrix products, arithmetic and copies ran while one was open for 2% -> 2% of each run, Pallas kernels for 11% -> 10%
where the time goes in v5:
time: 115 us
  starting transfers between devices  65.5 us (57%)
  waiting for transfers between devices  32.3 us (28%)
  Pallas kernels  14.1 us (12%)
  local copies, waits for them, and re-layouts  1.61 us (1%)
    ppermute x5, starting transfers between devices, along(): return lax.ppermute(x, ('z', 'core'), pairs)  25 us
    all_to_all x3, waiting for transfers between devices, body(): lax.all_to_all(result, ('y', 'core'), 0, 0, tiled=True).reshape(-1, FP, 128)  19.2 us
    all_to_all x3, starting transfers between devices, body(): lax.all_to_all(result, ('y', 'core'), 0, 0, tiled=True).reshape(-1, FP, 128)  18.1 us
    ppermute x4, starting transfers between devices, shift(): return lax.ppermute(x, axis, [(i, (i + by) % size) for i in range(size)])  17.9 us
    ppermute x5, waiting for transfers between devices, along(): return lax.ppermute(x, ('z', 'core'), pairs)  7.74 us
    pallas_call x6, Pallas kernels, body(): pl.pallas_call(functools.partial(result_kernel, mine, halves, lo - low),...  7.55 us
    all_to_all x1, starting transfers between devices, body(): request = lax.all_to_all(request, ('y', 'core'), 0, 0, tiled=True)  4.59 us
    all_to_all x1, waiting for transfers between devices, body(): request = lax.all_to_all(request, ('y', 'core'), 0, 0, tiled=True)  4.42 us
  transfers between devices with their start and end apart: 13, of which 7 were waited for; matrix products, arithmetic and copies ran while one was open for 2% of the time, Pallas kernels for 10%

profile of v5, /device:TPU:1, one launch (start us, length us, event | category | flops | bytes accessed | tf_op | source)
XLA Modules:
  0.0 114.6 jit_solution(4998188682527708018)
XLA Ops:
  0.0 5.6 %collective-permute-start = (bf16[144,576]{1,0:T(8,128)(2,1)}, bf16[144,576]{1,0:T(8,128)(2,1)S(1)}, u32[]{:S(2)}, u32[]{:S(2)}) collective-permute-start(bf16[144,576]{1,0:T(8,128)(2,1)} %k0), channel_id=1, source_target_pairs={{0,2},{1,3},{2,0},{3,1},{4,6},{5,7},{6,4},{7,5},{8,10},{9,11},{10,... | collective-permute-start | bytes 497672 | tf_op jit(solution)/shard_map/ppermute | solution.py:198
  5.6 2.2 %collective-permute-start.1 = (bf16[144,576]{1,0:T(8,128)(2,1)}, bf16[144,576]{1,0:T(8,128)(2,1)S(1)}, u32[]{:S(2)}, u32[]{:S(2)}) collective-permute-start(bf16[144,576]{1,0:T(8,128)(2,1)} %k0), channel_id=1, source_target_pairs={{0,1},{1,2},{2,3},{3,0},{4,5},{5,6},{6,7},{7,4},{8,9},{9,10},{10,1... | collective-permute-start | bytes 497672 | tf_op jit(solution)/shard_map/ppermute | solution.py:198
  7.8 4.3 %collective-permute-start.2 = (bf16[144,576]{1,0:T(8,128)(2,1)}, bf16[144,576]{1,0:T(8,128)(2,1)S(1)}, u32[]{:S(2)}, u32[]{:S(2)}) collective-permute-start(bf16[144,576]{1,0:T(8,128)(2,1)} %k0), channel_id=1, source_target_pairs={{0,3},{1,0},{2,1},{3,2},{4,7},{5,4},{6,5},{7,6},{8,11},{9,8},{10,9... | collective-permute-start | bytes 497672 | tf_op jit(solution)/shard_map/ppermute | solution.py:198
  12.8 1.0 fusion
  14.2 0.2 convert_element_type.6.coef_ref
  14.5 1.6 %request.1 = (bf16[8,2,16,768]{3,2,1,0:T(8,128)(2,1)}, s32[1,144]{1,0:T(1,128)S(1)}) custom-call(s32[1]{0:T(128)} %bitcast.z_ref, s32[1,144]{1,0:T(1,128)S(1)} %bitcast.20, f32[144,96]{1,0:T(8,128)S(1)} %copy.15.conduction_ref, f32[144,96]{1,0:T(8,128)S(1)} %copy.16.valence_ref), custom_call_target="tpu_custom_call" | custom-call | tf_op jit(solution)/shard_map/request/pallas_call | solution.py:215
  16.1 0.5 strip.1
  16.7 5.8 %collective-permute-start.3 = (bf16[2,144,128]{2,1,0:T(8,128)(2,1)S(1)}, bf16[2,144,128]{2,1,0:T(8,128)(2,1)S(1)}, u32[]{:S(2)}, u32[]{:S(2)}) collective-permute-start(bf16[2,144,128]{2,1,0:T(8,128)(2,1)S(1)} %strip.1), channel_id=1, source_target_pairs={{0,4},{4,0},{1,5},{5,1},{2,6},{6,2},{3,7},{7,3},{8,12},{12,8},{9,1... | collective-permute-start | bytes 221192 | tf_op jit(solution)/shard_map/ppermute | solution.py:198
  22.5 0.9 collective-permute-done.3
  23.4 8.8 %collective-permute-start.4 = (bf16[4,144,128]{2,1,0:T(8,128)(2,1)S(1)}, bf16[4,144,128]{2,1,0:T(8,128)(2,1)S(1)}, u32[]{:S(2)}, u32[]{:S(2)}) collective-permute-start(bf16[4,144,128]{2,1,0:T(8,128)(2,1)S(1)} %pad_maximum_fusion.1.refs_2_), channel_id=1, source_target_pairs={{0,8},{4,124},{8,16},{12,4},{16,24},{20,12},{24,32},{28,20},{32,40... | collective-permute-start | bytes 442376 | tf_op jit(solution)/shard_map/ppermute | solution.py:203
  32.2 4.6 %all-to-all-start = ((bf16[8,2,16,768]{3,2,1,0:T(8,128)(2,1)}), bf16[8,2,16,768]{3,2,1,0:T(8,128)(2,1)S(1)}, u32[]{:S(2)}, u32[]{:S(2)}) async-start(bf16[8,2,16,768]{3,2,1,0:T(8,128)(2,1)} %get-tuple-element.34), calls=%async_computation | async-start | bytes 786432 | tf_op jit(solution)/shard_map/all_to_all | solution.py:232
  36.8 3.6 %collective-permute-start.5 = (bf16[8,144,128]{2,1,0:T(8,128)(2,1)S(1)}, bf16[8,144,128]{2,1,0:T(8,128)(2,1)S(1)}, u32[]{:S(2)}, u32[]{:S(2)}) collective-permute-start(bf16[8,144,128]{2,1,0:T(8,128)(2,1)S(1)} %pad_maximum_fusion), channel_id=1, source_target_pairs={{0,16},{4,116},{8,24},{12,124},{16,32},{20,4},{24,40},{28,12},{32,... | collective-permute-start | bytes 884744 | tf_op jit(solution)/shard_map/ppermute | solution.py:203
  40.4 4.4 %all-to-all-done.x_ref = bf16[8,2,16,768]{3,2,1,0:T(8,128)(2,1)S(1)} async-done(((bf16[8,2,16,768]{3,2,1,0:T(8,128)(2,1)}), bf16[8,2,16,768]{3,2,1,0:T(8,128)(2,1)S(1)}, u32[]{:S(2)}, u32[]{:S(2)}) %all-to-all-start) | async-done | bytes 393248 | tf_op jit(solution)/shard_map/all_to_all | solution.py:232
  44.8 1.9 %expand.1 = (f32[8,96,128]{2,1,0:T(8,128)S(1)}, f32[8,96,128]{2,1,0:T(8,128)S(1)}, f32[8,96,128]{2,1,0:T(8,128)S(1)}, f32[8,96,128]{2,1,0:T(8,128)S(1)}, f32[16,1024]{1,0:T(8,128)S(1)}) custom-call(bf16[8,2,16,768]{3,2,1,0:T(8,128)(2,1)S(1)} %all-to-all-done.x_ref), custom_call_target="tpu_custom_call" | custom-call | tf_op jit(solution)/shard_map/expand/pallas_call | solution.py:234
  46.7 1.3 %result.6.refs_3_ = bf16[8,5,64,128]{3,2,1,0:T(8,128)(2,1)} custom-call(f32[16,1024]{1,0:T(8,128)S(1)} %get-tuple-element.53.local_ref, f32[8,96,128]{2,1,0:T(8,128)S(1)} %get-tuple-element.36.refs_0_, f32[8,96,128]{2,1,0:T(8,128)S(1)} %get-tuple-element.37.refs_1_, bf16[4,144,128]{2,1,0:T(8,128)(2,1)S(1)} %pad_maximum_fusion.1.refs_2_, ...), custom_call_target="tpu_custom_call" | custom-call | bytes 1000000 | tf_op jit(solution)/shard_map/result/pallas_call | solution.py:276
  48.0 3.8 %collective-permute-start.6 = (bf16[8,144,128]{2,1,0:T(8,128)(2,1)S(1)}, bf16[8,144,128]{2,1,0:T(8,128)(2,1)S(1)}, u32[]{:S(2)}, u32[]{:S(2)}) collective-permute-start(bf16[8,144,128]{2,1,0:T(8,128)(2,1)S(1)} %collective-permute-done.5.refs_2_), channel_id=1, source_target_pairs={{0,16},{4,116},{8,24},{12,124},{16,32},{20,4},{24,40},{28,12},{32,... | collective-permute-start | bytes 884744 | tf_op jit(solution)/shard_map/ppermute | solution.py:203
  51.8 1.2 %result.7 = bf16[8,5,64,128]{3,2,1,0:T(8,128)(2,1)} custom-call(f32[16,1024]{1,0:T(8,128)S(1)} %get-tuple-element.53.local_ref, f32[8,96,128]{2,1,0:T(8,128)S(1)} %get-tuple-element.36.refs_0_, f32[8,96,128]{2,1,0:T(8,128)S(1)} %get-tuple-element.37.refs_1_, bf16[8,144,128]{2,1,0:T(8,128)(2,1)S(1)} %collective-permute-done.5.refs_2_, ...), custom_call_target="tpu_custom_call", output_to_operand_aliasing={{}: (4, {})} | custom-call | flops 10000000000 | bytes 1000000 | tf_op jit(solution)/shard_map/result/pallas_call | solution.py:276
  53.0 1.2 %result.8.refs_5_ = bf16[8,6,64,128]{3,2,1,0:T(8,128)(2,1)} custom-call(f32[16,1024]{1,0:T(8,128)S(1)} %get-tuple-element.53.local_ref, f32[8,96,128]{2,1,0:T(8,128)S(1)} %get-tuple-element.36.refs_0_, f32[8,96,128]{2,1,0:T(8,128)S(1)} %get-tuple-element.37.refs_1_, bf16[8,144,128]{2,1,0:T(8,128)(2,1)S(1)} %collective-permute-done.5.refs_2_), custom_call_target="tpu_custom_call" | custom-call | bytes 1000000 | tf_op jit(solution)/shard_map/result/pallas_call | solution.py:276
  54.2 4.6 %all-to-all-start.1 = ((bf16[8,5,64,128]{3,2,1,0:T(8,128)(2,1)}), bf16[8,5,64,128]{3,2,1,0:T(8,128)(2,1)S(1)}, u32[]{:S(2)}, u32[]{:S(2)}) async-start(bf16[8,5,64,128]{3,2,1,0:T(8,128)(2,1)} %result.7), calls=%async_computation.1 | async-start | bytes 1310720 | tf_op jit(solution)/shard_map/all_to_all | solution.py:292
  58.7 1.0 collective-permute-done.6.refs_4_
  59.8 1.4 %result.9 = bf16[8,6,64,128]{3,2,1,0:T(8,128)(2,1)} custom-call(f32[16,1024]{1,0:T(8,128)S(1)} %get-tuple-element.53.local_ref, f32[8,96,128]{2,1,0:T(8,128)S(1)} %get-tuple-element.36.refs_0_, f32[8,96,128]{2,1,0:T(8,128)S(1)} %get-tuple-element.37.refs_1_, f32[8,96,128]{2,1,0:T(8,128)S(1)} %get-tuple-element.46.refs_2_.refs_0_, ...), custom_call_target="tpu_custom_call", output_to_operand_aliasing={{}: (6, {})} | custom-call | flops 20000000000 | bytes 1000000 | tf_op jit(solution)/shard_map/result/pallas_call | solution.py:276
  61.2 8.4 %all-to-all-done.1 = bf16[8,5,64,128]{3,2,1,0:T(8,128)(2,1)S(1)} async-done(((bf16[8,5,64,128]{3,2,1,0:T(8,128)(2,1)}), bf16[8,5,64,128]{3,2,1,0:T(8,128)(2,1)S(1)}, u32[]{:S(2)}, u32[]{:S(2)}) %all-to-all-start.1) | async-done | bytes 655392 | tf_op jit(solution)/shard_map/all_to_all | solution.py:292
  69.6 4.3 %all-to-all-start.2 = ((bf16[8,6,64,128]{3,2,1,0:T(8,128)(2,1)}), bf16[8,6,64,128]{3,2,1,0:T(8,128)(2,1)S(1)}, u32[]{:S(2)}, u32[]{:S(2)}) async-start(bf16[8,6,64,128]{3,2,1,0:T(8,128)(2,1)} %result.9), calls=%async_computation.2 | async-start | bytes 1572864 | tf_op jit(solution)/shard_map/all_to_all | solution.py:292
  74.0 5.4 %collective-permute-start.7 = (bf16[8,144,128]{2,1,0:T(8,128)(2,1)S(1)}, bf16[8,144,128]{2,1,0:T(8,128)(2,1)S(1)}, u32[]{:S(2)}, u32[]{:S(2)}) collective-permute-start(bf16[8,144,128]{2,1,0:T(8,128)(2,1)S(1)} %collective-permute-done.6.refs_4_), channel_id=1, source_target_pairs={{0,16},{4,116},{8,24},{12,124},{16,32},{20,4},{24,40},{28,12},{32,... | collective-permute-start | bytes 884744 | tf_op jit(solution)/shard_map/ppermute | solution.py:203
  79.4 6.5 %collective-permute-done.7.refs_2_ = bf16[8,144,128]{2,1,0:T(8,128)(2,1)S(1)} collective-permute-done((bf16[8,144,128]{2,1,0:T(8,128)(2,1)S(1)}, bf16[8,144,128]{2,1,0:T(8,128)(2,1)S(1)}, u32[]{:S(2)}, u32[]{:S(2)}) %collective-permute-start.7) | collective-permute-done | bytes 294944 | tf_op jit(solution)/shard_map/ppermute | solution.py:203
  85.9 3.4 %collective-permute-start.8 = (bf16[2,144,128]{2,1,0:T(8,128)(2,1)S(1)}, bf16[2,144,128]{2,1,0:T(8,128)(2,1)S(1)}, u32[]{:S(2)}, u32[]{:S(2)}) collective-permute-start(bf16[2,144,128]{2,1,0:T(8,128)(2,1)S(1)} %slice.20), channel_id=1, source_target_pairs={{0,8},{4,124},{8,16},{12,4},{16,24},{20,12},{24,32},{28,20},{32,40... | collective-permute-start | bytes 221192 | tf_op jit(solution)/shard_map/ppermute | solution.py:203
  89.2 1.5 %result.10.refs_3_ = bf16[8,5,64,128]{3,2,1,0:T(8,128)(2,1)} custom-call(f32[16,1024]{1,0:T(8,128)S(1)} %get-tuple-element.53.local_ref, f32[8,96,128]{2,1,0:T(8,128)S(1)} %get-tuple-element.46.refs_2_.refs_0_, f32[8,96,128]{2,1,0:T(8,128)S(1)} %get-tuple-element.47.refs_3_.refs_1_, bf16[8,144,128]{2,1,0:T(8,128)(2,1)S(1)} %collective-permute-done.7.refs_2_), custom_call_target="tpu_custom_call" | custom-call | flops 4000000000 | bytes 1000000 | tf_op jit(solution)/shard_map/result/pallas_call | solution.py:276
  90.7 0.3 collective-permute-done.8.refs_2_
  90.9 1.0 result.11
  92.0 9.2 %all-to-all-start.3 = ((bf16[8,5,64,128]{3,2,1,0:T(8,128)(2,1)}), bf16[8,5,64,128]{3,2,1,0:T(8,128)(2,1)S(1)}, u32[]{:S(2)}, u32[]{:S(2)}) async-start(bf16[8,5,64,128]{3,2,1,0:T(8,128)(2,1)} %result.11), calls=%async_computation.3 | async-start | bytes 1310720 | tf_op jit(solution)/shard_map/all_to_all | solution.py:292
  101.3 10.8 %all-to-all-done.3 = bf16[8,5,64,128]{3,2,1,0:T(8,128)(2,1)S(1)} async-done(((bf16[8,5,64,128]{3,2,1,0:T(8,128)(2,1)}), bf16[8,5,64,128]{3,2,1,0:T(8,128)(2,1)S(1)}, u32[]{:S(2)}, u32[]{:S(2)}) %all-to-all-start.3) | async-done | bytes 655392 | tf_op jit(solution)/shard_map/all_to_all | solution.py:292
  112.1 2.5 %assemble.1 = bf16[64,9216]{1,0:T(8,128)(2,1)} custom-call(s32[144]{0:T(256)S(1)} %bitcast.21, s32[1]{0:T(128)} %bitcast.3.where_ref, bf16[40,64,128]{2,1,0:T(8,128)(2,1)S(1)} %bitcast.18, bf16[48,64,128]{2,1,0:T(8,128)(2,1)S(1)} %bitcast.17, bf16[40,64,128]{2,1,0:T(8,128)(2,1)S(1)} %bitcast.19, f32[64,1]{1,0:T(8,128)S(1)} %copy.17.refs_3_), custom_call_target="tpu_custom_call" | custom-call | tf_op jit(solution)/shard_map/assemble/pallas_call | solution.py:295
  (26 shorter events, 0.6 us)
Async XLA Ops:
  0.0 14.1 %copy-start.2 = (f32[2,1,8,12]{3,2,1,0:T(8,128)S(1)}, f32[2,1,8,12]{3,2,1,0:T(8,128)}, u32[]{:S(2)}) copy-start(f32[2,1,8,12]{3,2,1,0:T(8,128)} %param.7) | copy-start | bytes 2308
  0.0 14.5 %copy-start.1 = (s32[144]{0:T(256)S(1)}, s32[144]{0:T(256)}, u32[]{:S(2)}) copy-start(s32[144]{0:T(256)} %param.10) | copy-start | bytes 1732
  0.0 16.1 %collective-permute-start = (bf16[144,576]{1,0:T(8,128)(2,1)}, bf16[144,576]{1,0:T(8,128)(2,1)S(1)}, u32[]{:S(2)}, u32[]{:S(2)}) collective-permute-start(bf16[144,576]{1,0:T(8,128)(2,1)} %k0), channel_id=1, source_target_pairs={{0,2},{1,3},{2,0},{3,1},{4,6},{5,7},{6,4},{7,5},{8,10},{9,11},{10,... | collective-permute-start | bytes 497672 | tf_op jit(solution)/shard_map/ppermute | solution.py:198
  5.6 10.5 %collective-permute-start.1 = (bf16[144,576]{1,0:T(8,128)(2,1)}, bf16[144,576]{1,0:T(8,128)(2,1)S(1)}, u32[]{:S(2)}, u32[]{:S(2)}) collective-permute-start(bf16[144,576]{1,0:T(8,128)(2,1)} %k0), channel_id=1, source_target_pairs={{0,1},{1,2},{2,3},{3,0},{4,5},{5,6},{6,7},{7,4},{8,9},{9,10},{10,1... | collective-permute-start | bytes 497672 | tf_op jit(solution)/shard_map/ppermute | solution.py:198
  7.8 8.3 %collective-permute-start.2 = (bf16[144,576]{1,0:T(8,128)(2,1)}, bf16[144,576]{1,0:T(8,128)(2,1)S(1)}, u32[]{:S(2)}, u32[]{:S(2)}) collective-permute-start(bf16[144,576]{1,0:T(8,128)(2,1)} %k0), channel_id=1, source_target_pairs={{0,3},{1,0},{2,1},{3,2},{4,7},{5,4},{6,5},{7,6},{8,11},{9,8},{10,9... | collective-permute-start | bytes 497672 | tf_op jit(solution)/shard_map/ppermute | solution.py:198
  12.8 3.4 %copy-start = (bf16[144,576]{1,0:T(8,128)(2,1)S(1)}, bf16[144,576]{1,0:T(8,128)(2,1)}, u32[]{:S(2)}) copy-start(bf16[144,576]{1,0:T(8,128)(2,1)} %k0) | copy-start | bytes 497668
  16.7 6.7 %collective-permute-start.3 = (bf16[2,144,128]{2,1,0:T(8,128)(2,1)S(1)}, bf16[2,144,128]{2,1,0:T(8,128)(2,1)S(1)}, u32[]{:S(2)}, u32[]{:S(2)}) collective-permute-start(bf16[2,144,128]{2,1,0:T(8,128)(2,1)S(1)} %strip.1), channel_id=1, source_target_pairs={{0,4},{4,0},{1,5},{5,1},{2,6},{6,2},{3,7},{7,3},{8,12},{12,8},{9,1... | collective-permute-start | bytes 221192 | tf_op jit(solution)/shard_map/ppermute | solution.py:198
  23.4 13.4 %collective-permute-start.4 = (bf16[4,144,128]{2,1,0:T(8,128)(2,1)S(1)}, bf16[4,144,128]{2,1,0:T(8,128)(2,1)S(1)}, u32[]{:S(2)}, u32[]{:S(2)}) collective-permute-start(bf16[4,144,128]{2,1,0:T(8,128)(2,1)S(1)} %pad_maximum_fusion.1.refs_2_), channel_id=1, source_target_pairs={{0,8},{4,124},{8,16},{12,4},{16,24},{20,12},{24,32},{28,20},{32,40... | collective-permute-start | bytes 442376 | tf_op jit(solution)/shard_map/ppermute | solution.py:203
  32.2 12.7 %all-to-all-start = ((bf16[8,2,16,768]{3,2,1,0:T(8,128)(2,1)}), bf16[8,2,16,768]{3,2,1,0:T(8,128)(2,1)S(1)}, u32[]{:S(2)}, u32[]{:S(2)}) async-start(bf16[8,2,16,768]{3,2,1,0:T(8,128)(2,1)} %get-tuple-element.34), calls=%async_computation | async-start | bytes 786432 | tf_op jit(solution)/shard_map/all_to_all | solution.py:232
  36.8 11.2 %collective-permute-start.5 = (bf16[8,144,128]{2,1,0:T(8,128)(2,1)S(1)}, bf16[8,144,128]{2,1,0:T(8,128)(2,1)S(1)}, u32[]{:S(2)}, u32[]{:S(2)}) collective-permute-start(bf16[8,144,128]{2,1,0:T(8,128)(2,1)S(1)} %pad_maximum_fusion), channel_id=1, source_target_pairs={{0,16},{4,116},{8,24},{12,124},{16,32},{20,4},{24,40},{28,12},{32,... | collective-permute-start | bytes 884744 | tf_op jit(solution)/shard_map/ppermute | solution.py:203
  48.0 11.7 %collective-permute-start.6 = (bf16[8,144,128]{2,1,0:T(8,128)(2,1)S(1)}, bf16[8,144,128]{2,1,0:T(8,128)(2,1)S(1)}, u32[]{:S(2)}, u32[]{:S(2)}) collective-permute-start(bf16[8,144,128]{2,1,0:T(8,128)(2,1)S(1)} %collective-permute-done.5.refs_2_), channel_id=1, source_target_pairs={{0,16},{4,116},{8,24},{12,124},{16,32},{20,4},{24,40},{28,12},{32,... | collective-permute-start | bytes 884744 | tf_op jit(solution)/shard_map/ppermute | solution.py:203
  54.2 15.5 %all-to-all-start.1 = ((bf16[8,5,64,128]{3,2,1,0:T(8,128)(2,1)}), bf16[8,5,64,128]{3,2,1,0:T(8,128)(2,1)S(1)}, u32[]{:S(2)}, u32[]{:S(2)}) async-start(bf16[8,5,64,128]{3,2,1,0:T(8,128)(2,1)} %result.7), calls=%async_computation.1 | async-start | bytes 1310720 | tf_op jit(solution)/shard_map/all_to_all | solution.py:292
  69.6 22.4 %all-to-all-start.2 = ((bf16[8,6,64,128]{3,2,1,0:T(8,128)(2,1)}), bf16[8,6,64,128]{3,2,1,0:T(8,128)(2,1)S(1)}, u32[]{:S(2)}, u32[]{:S(2)}) async-start(bf16[8,6,64,128]{3,2,1,0:T(8,128)(2,1)} %result.9), calls=%async_computation.2 | async-start | bytes 1572864 | tf_op jit(solution)/shard_map/all_to_all | solution.py:292
  74.0 11.9 %collective-permute-start.7 = (bf16[8,144,128]{2,1,0:T(8,128)(2,1)S(1)}, bf16[8,144,128]{2,1,0:T(8,128)(2,1)S(1)}, u32[]{:S(2)}, u32[]{:S(2)}) collective-permute-start(bf16[8,144,128]{2,1,0:T(8,128)(2,1)S(1)} %collective-permute-done.6.refs_4_), channel_id=1, source_target_pairs={{0,16},{4,116},{8,24},{12,124},{16,32},{20,4},{24,40},{28,12},{32,... | collective-permute-start | bytes 884744 | tf_op jit(solution)/shard_map/ppermute | solution.py:203
  85.9 5.1 %collective-permute-start.8 = (bf16[2,144,128]{2,1,0:T(8,128)(2,1)S(1)}, bf16[2,144,128]{2,1,0:T(8,128)(2,1)S(1)}, u32[]{:S(2)}, u32[]{:S(2)}) collective-permute-start(bf16[2,144,128]{2,1,0:T(8,128)(2,1)S(1)} %slice.20), channel_id=1, source_target_pairs={{0,8},{4,124},{8,16},{12,4},{16,24},{20,12},{24,32},{28,20},{32,40... | collective-permute-start | bytes 221192 | tf_op jit(solution)/shard_map/ppermute | solution.py:203
  92.0 9.2 %copy-start.3 = (f32[64]{0:T(128)S(1)}, f32[64]{0:T(128)}, u32[]{:S(2)}) copy-start(f32[64]{0:T(128)} %param.11) | copy-start | bytes 772
  92.0 20.1 %all-to-all-start.3 = ((bf16[8,5,64,128]{3,2,1,0:T(8,128)(2,1)}), bf16[8,5,64,128]{3,2,1,0:T(8,128)(2,1)S(1)}, u32[]{:S(2)}, u32[]{:S(2)}) async-start(bf16[8,5,64,128]{3,2,1,0:T(8,128)(2,1)} %result.11), calls=%async_computation.3 | async-start | bytes 1310720 | tf_op jit(solution)/shard_map/all_to_all | solution.py:292
